TPU v7x, 32 devices: a whole 2x2x4 slice. The times are simulated.
32 devices in a mesh: dp: 8 (over y, x, core), tensor: 4 (over z).
Axes of the slice: x: 2, y: 2, z: 4, core: 2. Of those that a mesh axis runs over, the one named last changes fastest.
Arguments:
- tokens: bfloat16 [580, 8, 1024], P('tensor', 'dp'), may hold values from -6 to 6
- ln1_gain: bfloat16 [1024], P('dp'), may hold values from 0.099609375 to 1.8984375
- ln1_bias: bfloat16 [1024], P('dp'), may hold values from -1.5 to 1.5
- w_qkv: bfloat16 [3, 1024, 1024], P(None, 'dp', 'tensor'), may hold values from -0.1875 to 0.1875
- b_qv: bfloat16 [2, 1024], P(None, 'dp'), may hold values from -1.5 to 1.5
- w_out: bfloat16 [1024, 1024], P('tensor', 'dp'), may hold values from -0.75 to 0.75
- b_out: bfloat16 [1024], P('dp'), may hold values from -1.5 to 1.5
- ln2_gain: bfloat16 [1024], P('dp'), may hold values from 0.099609375 to 1.8984375
- ln2_bias: bfloat16 [1024], P('dp'), may hold values from -1.5 to 1.5
- w_up: bfloat16 [1024, 4096], P('dp', 'tensor'), may hold values from -0.1875 to 0.1875
- b_up: bfloat16 [4096], P('dp'), may hold values from -2.5 to 2.5
- w_down: bfloat16 [4096, 1024], P('tensor', 'dp'), may hold values from -0.09375 to 0.09375
- b_down: bfloat16 [1024], P('dp'), may hold values from -1.5 to 1.5
- cotangent: bfloat16 [580, 8, 1024], P('tensor', 'dp'), may hold values from -6 to 6
Outputs:
- mixed: bfloat16 [580, 8, 1024], P('tensor', 'dp')
- grad_tokens: float32 [580, 8, 1024], P('tensor', 'dp')
- grad_ln1_gain: float32 [1024], P('dp')
- grad_ln1_bias: float32 [1024], P('dp')
- grad_w_qkv: float32 [3, 1024, 1024], P(None, 'dp', 'tensor')
- grad_b_qv: float32 [2, 1024], P(None, 'dp')
- grad_w_out: float32 [1024, 1024], P('tensor', 'dp')
- grad_b_out: float32 [1024], P('dp')
- grad_ln2_gain: float32 [1024], P('dp')
- grad_ln2_bias: float32 [1024], P('dp')
- grad_w_up: float32 [1024, 4096], P('dp', 'tensor')
- grad_b_up: float32 [4096], P('dp')
- grad_w_down: float32 [4096, 1024], P('tensor', 'dp')
- grad_b_down: float32 [1024], P('dp')
All inputs are finite; a program needn't handle non-finite values.
Results may differ from a plain program's by a relative error of at most 0.017.
Values may be sent and summed in bfloat16 or wider, within the bound.
A program may use at most 128 MiB of HBM per device.

v0:
```python
import math

import jax
import jax.numpy as jnp
from jax import lax
from jax.sharding import PartitionSpec as P

HEAD_DIM = 64
SEQ = 577


EPS = 1e-06
NEG = -1000000000.0


def cut_along(value, dim, size):
    lengths = value.shape
    parts = value.reshape(*lengths[:dim], size, lengths[dim] // size, *lengths[dim + 1 :])
    return jnp.moveaxis(parts, dim, 0)


def sent_and_summed(value, axis, dim):
    size = lax.axis_size(axis)
    parts = lax.all_to_all(cut_along(value, dim, size), axis, 0, 0, tiled=True)
    return jnp.sum(parts.astype(jnp.float32), axis=0)


def sent_together(arrays, axis, dim, along):
    ends, at = ([], 0)
    for a in arrays[:-1]:
        at += a.shape[along]
        ends.append(at)
    both = jnp.concatenate(arrays, axis=along)
    return tuple(jnp.split(sent_and_summed(both, axis, dim), ends, axis=along))


def layer_norm(values, gain, shift):
    center = values - jnp.mean(values, axis=-1, keepdims=True)
    spread = jnp.mean(center * center, axis=-1, keepdims=True)
    return center * lax.rsqrt(spread + EPS) * gain + shift


def exact_gelu(values):
    return jax.nn.gelu(values, approximate=False)


def body(
    tokens,
    ln1_gain,
    ln1_bias,
    w_qkv,
    b_qv,
    w_out,
    b_out,
    ln2_gain,
    ln2_bias,
    w_up,
    b_up,
    w_down,
    b_down,
    cotangent,
):
    slot = tokens.shape[0]
    images = tokens.shape[1]
    parts = lax.axis_size("tensor")
    member = lax.axis_index("tensor")
    total = slot * parts
    positions = member * slot + jnp.arange(slot, dtype=jnp.int32)
    live_rows = positions < SEQ
    key_live = jnp.arange(total, dtype=jnp.int32) < SEQ
    scale = 1.0 / math.sqrt(HEAD_DIM)
    qkv_full, out_full, qv_bias, gain_one, shift_one, out_bias = (
        lax.all_gather(w_qkv, "dp", axis=1, tiled=True),
        lax.all_gather(w_out, "dp", axis=1, tiled=True),
        lax.all_gather(b_qv, "dp", axis=1, tiled=True),
        lax.all_gather(ln1_gain, "dp", axis=0, tiled=True),
        lax.all_gather(ln1_bias, "dp", axis=0, tiled=True),
        lax.all_gather(b_out, "dp", axis=0, tiled=True),
    )
    local_width = qkv_full.shape[2]
    heads_here = local_width // HEAD_DIM
    head_start = member * local_width
    own_bias = lax.dynamic_slice_in_dim(qv_bias, head_start, local_width, 1).astype(jnp.float32)
    gain_one = gain_one.astype(jnp.float32)
    shift_one = shift_one.astype(jnp.float32)

    def split_heads(values):
        return values.reshape(total, images, heads_here, HEAD_DIM)

    def scores_of(query_rows, key_rows):
        raw = (
            jnp.einsum(
                "qihe,kihe->ihqk",
                split_heads(query_rows),
                split_heads(key_rows),
                preferred_element_type=jnp.float32,
            )
            * scale
        )
        return jnp.where(key_live[None, None, None, :], raw, NEG)

    inputs = tokens.astype(jnp.float32)
    normed_one = layer_norm(inputs, gain_one, shift_one).astype(jnp.bfloat16)
    attn_rows = lax.all_gather(normed_one, "tensor", axis=0, tiled=True)
    projected = jnp.einsum("pid,cde->cpie", attn_rows, qkv_full, preferred_element_type=jnp.float32)
    queries = (projected[0] + own_bias[0]).astype(jnp.bfloat16)
    keys = projected[1].astype(jnp.bfloat16)
    values = (projected[2] + own_bias[1]).astype(jnp.bfloat16)
    scores = scores_of(queries, keys)
    top = jnp.max(scores, axis=-1, keepdims=True)
    expo = jnp.exp(scores - top)
    denom = jnp.sum(expo, axis=-1, keepdims=True)
    probs = expo / denom
    log_total = top + jnp.log(denom)
    mixed_heads = (
        jnp.einsum(
            "ihqk,kihe->qihe",
            probs.astype(jnp.bfloat16),
            split_heads(values),
            preferred_element_type=jnp.float32,
        )
        .reshape(total, images, local_width)
        .astype(jnp.bfloat16)
    )
    rows = mixed_heads
    branch = lax.psum_scatter(
        jnp.einsum("pie,ed->pid", rows, out_full, preferred_element_type=jnp.float32).astype(
            jnp.bfloat16
        ),
        "tensor",
        scatter_dimension=0,
        tiled=True,
    ).astype(jnp.float32) + out_bias.astype(jnp.float32)
    first = inputs + branch
    up_full, down_full, up_bias, gain_two, shift_two, down_bias = (
        lax.all_gather(w_up, "dp", axis=0, tiled=True),
        lax.all_gather(w_down, "dp", axis=1, tiled=True),
        lax.all_gather(b_up, "dp", axis=0, tiled=True),
        lax.all_gather(ln2_gain, "dp", axis=0, tiled=True),
        lax.all_gather(ln2_bias, "dp", axis=0, tiled=True),
        lax.all_gather(b_down, "dp", axis=0, tiled=True),
    )
    hidden_width = up_full.shape[1]
    hidden_start = member * hidden_width
    up_own = lax.dynamic_slice_in_dim(up_bias, hidden_start, hidden_width, 0).astype(jnp.float32)
    gain_two = gain_two.astype(jnp.float32)
    shift_two = shift_two.astype(jnp.float32)
    normed_two = layer_norm(first, gain_two, shift_two).astype(jnp.bfloat16)
    mlp_rows = lax.all_gather(normed_two, "tensor", axis=0, tiled=True)
    pre_act = (
        jnp.einsum("pid,df->pif", mlp_rows, up_full, preferred_element_type=jnp.float32) + up_own
    )
    activated = exact_gelu(pre_act).astype(jnp.bfloat16)
    rows = activated
    mixed = (
        first
        + lax.psum_scatter(
            jnp.einsum("pif,fd->pid", rows, down_full, preferred_element_type=jnp.float32).astype(
                jnp.bfloat16
            ),
            "tensor",
            scatter_dimension=0,
            tiled=True,
        ).astype(jnp.float32)
        + down_bias.astype(jnp.float32)
    ).astype(jnp.bfloat16)
    qkv_back, out_back, up_back, down_back = (
        lax.all_gather(w_qkv, "dp", axis=1, tiled=True),
        lax.all_gather(w_out, "dp", axis=1, tiled=True),
        lax.all_gather(w_up, "dp", axis=0, tiled=True),
        lax.all_gather(w_down, "dp", axis=1, tiled=True),
    )
    masked_grad = jnp.where(live_rows[:, None, None], cotangent, jnp.zeros_like(cotangent))
    grad_rows = lax.all_gather(masked_grad, "tensor", axis=0, tiled=True)
    grad_down = jnp.einsum("pif,pid->fd", activated, grad_rows, preferred_element_type=jnp.float32)
    grad_act = jnp.einsum("pid,fd->pif", grad_rows, down_back, preferred_element_type=jnp.float32)
    gelu_pull = jax.vjp(exact_gelu, pre_act)[1]
    grad_pre = gelu_pull(grad_act)[0].astype(jnp.bfloat16)
    grad_up = jnp.einsum("pid,pif->df", mlp_rows, grad_pre, preferred_element_type=jnp.float32)
    up_bias_part = jnp.sum(grad_pre.astype(jnp.float32), axis=(0, 1))
    up_bias_grad = lax.dynamic_update_slice_in_dim(
        jnp.zeros(up_bias.shape, jnp.float32), up_bias_part, hidden_start, 0
    )
    rows = grad_pre
    grad_normed_two = lax.psum_scatter(
        jnp.einsum("pif,df->pid", rows, up_back, preferred_element_type=jnp.float32).astype(
            jnp.bfloat16
        ),
        "tensor",
        scatter_dimension=0,
        tiled=True,
    ).astype(jnp.float32)
    norm_two_pull = jax.vjp(layer_norm, first, gain_two, shift_two)[1]
    grad_first_norm, grad_gain_two, grad_shift_two = norm_two_pull(grad_normed_two)
    masked_float = masked_grad.astype(jnp.float32)
    grad_down_bias = jnp.sum(masked_float, axis=(0, 1))
    up_w_sum, down_w_sum, up_b_sum, gain_two_sum, shift_two_sum, down_b_sum = (
        lax.psum_scatter(grad_up, "dp", scatter_dimension=0, tiled=True),
        lax.psum_scatter(grad_down, "dp", scatter_dimension=1, tiled=True),
        lax.psum_scatter(up_bias_grad, "dp", scatter_dimension=0, tiled=True),
        lax.psum_scatter(grad_gain_two, "dp", scatter_dimension=0, tiled=True),
        lax.psum_scatter(grad_shift_two, "dp", scatter_dimension=0, tiled=True),
        lax.psum_scatter(grad_down_bias, "dp", scatter_dimension=0, tiled=True),
    )
    grad_first = masked_float + grad_first_norm
    grad_branch = grad_first.astype(jnp.bfloat16)
    grad_out_bias = jnp.sum(grad_branch.astype(jnp.float32), axis=(0, 1))
    branch_rows = lax.all_gather(grad_branch, "tensor", axis=0, tiled=True)
    grad_out_w = jnp.einsum(
        "pie,pid->ed", mixed_heads, branch_rows, preferred_element_type=jnp.float32
    )
    grad_heads = jnp.einsum(
        "pid,ed->pie", branch_rows, out_back, preferred_element_type=jnp.float32
    ).astype(jnp.bfloat16)
    grad_split = split_heads(grad_heads)
    probs_again = jnp.exp(scores_of(queries, keys) - log_total)
    grad_probs = jnp.einsum(
        "qihe,kihe->ihqk", grad_split, split_heads(values), preferred_element_type=jnp.float32
    )
    grad_values = (
        jnp.einsum(
            "ihqk,qihe->kihe",
            probs_again.astype(jnp.bfloat16),
            grad_split,
            preferred_element_type=jnp.float32,
        )
        .reshape(total, images, local_width)
        .astype(jnp.bfloat16)
    )
    inner = jnp.sum(probs_again * grad_probs, axis=-1, keepdims=True)
    grad_scores = (probs_again * (grad_probs - inner)).astype(jnp.bfloat16)
    grad_queries = (
        (
            jnp.einsum(
                "ihqk,kihe->qihe",
                grad_scores,
                split_heads(keys),
                preferred_element_type=jnp.float32,
            )
            * scale
        )
        .reshape(total, images, local_width)
        .astype(jnp.bfloat16)
    )
    grad_keys = (
        (
            jnp.einsum(
                "ihqk,qihe->kihe",
                grad_scores,
                split_heads(queries),
                preferred_element_type=jnp.float32,
            )
            * scale
        )
        .reshape(total, images, local_width)
        .astype(jnp.bfloat16)
    )
    grad_qkv = jnp.stack([grad_queries, grad_keys, grad_values])
    grad_qkv_w = jnp.einsum(
        "pid,cpie->cde", attn_rows, grad_qkv, preferred_element_type=jnp.float32
    )
    qv_part = jnp.stack(
        [
            jnp.sum(grad_queries.astype(jnp.float32), axis=(0, 1)),
            jnp.sum(grad_values.astype(jnp.float32), axis=(0, 1)),
        ]
    )
    qv_grad = lax.dynamic_update_slice_in_dim(
        jnp.zeros(qv_bias.shape, jnp.float32), qv_part, head_start, 1
    )
    rows = grad_qkv
    grad_normed_one = lax.psum_scatter(
        jnp.einsum("cpie,cde->pid", rows, qkv_back, preferred_element_type=jnp.float32).astype(
            jnp.bfloat16
        ),
        "tensor",
        scatter_dimension=0,
        tiled=True,
    ).astype(jnp.float32)
    norm_one_pull = jax.vjp(layer_norm, inputs, gain_one, shift_one)[1]
    grad_inputs_norm, grad_gain_one, grad_shift_one = norm_one_pull(grad_normed_one)
    grad_tokens = grad_first + grad_inputs_norm
    qkv_w_sum, out_w_sum, qv_b_sum, gain_one_sum, shift_one_sum, out_b_sum = (
        sent_and_summed(grad_qkv_w.astype(jnp.bfloat16), "dp", 1),
        *sent_together((grad_out_w.astype(jnp.bfloat16), qv_grad.astype(jnp.bfloat16)), "dp", 1, 0),
        sent_and_summed(grad_gain_one.astype(jnp.bfloat16), "dp", 0),
        sent_and_summed(grad_shift_one.astype(jnp.bfloat16), "dp", 0),
        sent_and_summed(grad_out_bias.astype(jnp.bfloat16), "dp", 0),
    )
    (
        gain_one_total,
        shift_one_total,
        qv_b_total,
        out_b_total,
        gain_two_total,
        shift_two_total,
        up_b_total,
        down_b_total,
    ) = lax.psum(
        (
            gain_one_sum,
            shift_one_sum,
            qv_b_sum,
            out_b_sum,
            gain_two_sum,
            shift_two_sum,
            up_b_sum,
            down_b_sum,
        ),
        "tensor",
    )
    return (
        mixed,
        grad_tokens,
        gain_one_total,
        shift_one_total,
        qkv_w_sum,
        qv_b_total,
        out_w_sum,
        out_b_total,
        gain_two_total,
        shift_two_total,
        up_w_sum,
        up_b_total,
        down_w_sum,
        down_b_total,
    )


def solution(mesh):
    placed = (
        P("tensor", "dp", None),
        P("dp"),
        P("dp"),
        P(None, "dp", "tensor"),
        P(None, "dp"),
        P("tensor", "dp"),
        P("dp"),
        P("dp"),
        P("dp"),
        P("dp", "tensor"),
        P("dp"),
        P("tensor", "dp"),
        P("dp"),
        P("tensor", "dp", None),
    )
    return jax.shard_map(
        body,
        mesh=mesh,
        in_specs=placed,
        out_specs=(
            P("tensor", "dp", None),
            P("tensor", "dp", None),
            P("dp"),
            P("dp"),
            P(None, "dp", "tensor"),
            P(None, "dp"),
            P("tensor", "dp"),
            P("dp"),
            P("dp"),
            P("dp"),
            P("dp", "tensor"),
            P("dp"),
            P("tensor", "dp"),
            P("dp"),
        ),
        check_vma=False,
    )
```

profile of v0, /device:TPU:0, one launch (start us, length us, event | category | flops | bytes accessed | tf_op | source)
XLA Modules:
  0.0 569.7 jit_solution(10248400032738955662)
XLA Ops:
  9.3 10.3 %all-gather = bf16[8,1,128]{2,1,0:T(2,128)(2,1)S(1)} all-gather(bf16[1,1,128]{2,1,0:T(2,128)(2,1)} %bitcast.192), channel_id=1, replica_groups=mesh['dp'=8,'tensor'=4] {'dp'}, dimensions={0}, use_global_device_ids=true | all-gather | bytes 2304 | tf_op jit(solution)/shard_map/all_gather | solution.py:76
  19.6 8.6 %all-gather.1 = bf16[8,1,128]{2,1,0:T(2,128)(2,1)S(1)} all-gather(bf16[1,1,128]{2,1,0:T(2,128)(2,1)} %bitcast.193), channel_id=1, replica_groups=mesh['dp'=8,'tensor'=4] {'dp'}, dimensions={0}, use_global_device_ids=true | all-gather | bytes 2304 | tf_op jit(solution)/shard_map/all_gather | solution.py:77
  28.2 2.9 multiply_reduce_fusion.6
  35.1 7.9 %all_gather.56 = bf16[2,1024]{1,0:T(2,128)(2,1)S(1)} all-gather(bf16[2,128]{1,0:T(2,128)(2,1)S(1)} %copy-done.18), channel_id=1, replica_groups=mesh['dp'=8,'tensor'=4] {'dp'}, dimensions={1}, use_global_device_ids=true | all-gather | bytes 4608 | tf_op jit(solution)/shard_map/all_gather | solution.py:75
  43.1 9.8 %all_gather.57 = bf16[256,1024]{1,0:T(8,128)(2,1)S(1)} all-gather(bf16[256,128]{1,0:T(8,128)(2,1)S(1)} %copy-done.16), channel_id=1, replica_groups=mesh['dp'=8,'tensor'=4] {'dp'}, dimensions={1}, use_global_device_ids=true | all-gather | bytes 589824 | tf_op jit(solution)/shard_map/all_gather | solution.py:74
  53.0 31.7 %all-gather.15.cloned.1.call-done = bf16[580,1,1024]{2,1,0:T(2,128)(2,1)} async-done(((bf16[145,1,1024]{2,1,0:T(2,128)(2,1)}), bf16[580,1,1024]{2,1,0:T(2,128)(2,1)}) %all-gather.15.cloned.1.call-update) | async-done | bytes 1187856 | tf_op jit(solution)/shard_map/all_gather | solution.py:104
  84.7 26.4 %all-gather.17.cloned.1.call-done = bf16[3,1024,256]{2,1,0:T(8,128)(2,1)} async-done(((bf16[3,128,256]{2,1,0:T(8,128)(2,1)}), bf16[3,1024,256]{2,1,0:T(8,128)(2,1)}) %all-gather.17.cloned.1.call-update) | async-done | bytes 1572880 | tf_op jit(solution)/shard_map/all_gather | solution.py:73
  111.1 3.3 convolution_bitcast_fusion
  121.8 29.1 %fusion = bf16[152,1024]{1,0:T(8,128)(2,1)S(1)} fusion(bf16[580,1,1024]{2,0,1:T(8,128)(2,1)S(1)} %fusion.20), kind=kCustom, calls=%all-reduce-scatter | all-reduce-scatter fusion | flops 622593 | bytes 1499648
  152.3 8.7 %all-gather.2 = bf16[8,1,128]{2,1,0:T(2,128)(2,1)S(1)} all-gather(bf16[1,1,128]{2,1,0:T(2,128)(2,1)S(1)} %bitcast.194), channel_id=1, replica_groups=mesh['dp'=8,'tensor'=4] {'dp'}, dimensions={0}, use_global_device_ids=true | all-gather | bytes 2304 | tf_op jit(solution)/shard_map/all_gather | solution.py:78
  161.0 7.8 %all-gather.3 = bf16[8,1,128]{2,1,0:T(2,128)(2,1)S(1)} all-gather(bf16[1,1,128]{2,1,0:T(2,128)(2,1)S(1)} %bitcast.195), channel_id=1, replica_groups=mesh['dp'=8,'tensor'=4] {'dp'}, dimensions={0}, use_global_device_ids=true | all-gather | bytes 2304 | tf_op jit(solution)/shard_map/all_gather | solution.py:139
  168.8 9.2 %all-gather.4 = bf16[8,1,128]{2,1,0:T(2,128)(2,1)S(1)} all-gather(bf16[1,1,128]{2,1,0:T(2,128)(2,1)S(1)} %bitcast.196), channel_id=1, replica_groups=mesh['dp'=8,'tensor'=4] {'dp'}, dimensions={0}, use_global_device_ids=true | all-gather | bytes 2304 | tf_op jit(solution)/shard_map/all_gather | solution.py:140
  187.6 7.9 %all-gather.5 = bf16[8,1,512]{2,1,0:T(2,128)(2,1)S(1)} all-gather(bf16[1,1,512]{2,1,0:T(2,128)(2,1)S(1)} %reshape.567), channel_id=1, replica_groups=mesh['dp'=8,'tensor'=4] {'dp'}, dimensions={0}, use_global_device_ids=true | all-gather | bytes 9216 | tf_op jit(solution)/shard_map/all_gather | solution.py:138
  195.7 37.9 %all-gather.19.cloned.1.call-done = bf16[580,1,1024]{2,1,0:T(2,128)(2,1)} async-done(((bf16[145,1,1024]{2,1,0:T(2,128)(2,1)}), bf16[580,1,1024]{2,1,0:T(2,128)(2,1)}) %all-gather.19.cloned.1.call-update) | async-done | bytes 1187856 | tf_op jit(solution)/shard_map/all_gather | solution.py:149
  233.5 10.0 %multiply_convert_fusion.1 = (bf16[580,1024]{1,0:T(8,128)(2,1)}, f32[580,1024]{1,0:T(8,128)}, f32[580,1024]{1,0:T(8,128)}) fusion(f32[1024]{0:T(1024)S(1)} %dynamic-slice_convert_fusion, bf16[1024,1024]{1,0:T(8,128)(2,1)} %all-gather.21.cloned.1.call-done, bf16[580,1,1024]{2,1,0:T(2,128)(2,1)} %all-gather.19.cloned.1.call-done), kind=kOutput, calls=%fused_computation.17 | convolution fusion | flops 1255546880 | bytes 9228288 | tf_op jit(solution)/shard_map/pid,df->pif/dot_general | solution.py:151
  243.6 41.0 %all-gather.25.cloned.1.call-done = bf16[580,1,1024]{2,1,0:T(2,128)(2,1)} async-done(((bf16[145,1,1024]{2,1,0:T(2,128)(2,1)}), bf16[580,1,1024]{2,1,0:T(2,128)(2,1)}) %all-gather.25.cloned.1.call-update) | async-done | bytes 1187856 | tf_op jit(solution)/shard_map/all_gather | solution.py:174
  284.6 28.8 %all-gather.23.cloned.1.call-done = bf16[1024,1024]{1,0:T(8,128)(2,1)} async-done(((bf16[1024,128]{1,0:T(8,128)(2,1)}), bf16[1024,1024]{1,0:T(8,128)(2,1)}) %all-gather.23.cloned.1.call-update) | async-done | bytes 2097168 | tf_op jit(solution)/shard_map/all_gather | solution.py:137
  313.3 6.1 %convert_reduce_fusion.1 = (f32[1024]{0:T(1024)S(1)}, bf16[580,1024]{1,0:T(8,128)(2,1)S(1)}) fusion(f32[580,1024]{1,0:T(8,128)} %get-tuple-element.104, bf16[1024,1024]{1,0:T(8,128)(2,1)} %all-gather.23.cloned.1.call-done, bf16[580,1,1024]{2,1,0:T(2,128)(2,1)} %all-gather.25.cloned.1.call-done, f32[580,1024]{1,0:T(8,128)} %get-tuple-element.115, ...), kind=kOutput, calls=%fused_computation.15 | convolution fusion | flops 1226443776 | bytes 9232384 | tf_op jit(solution)/shard_map/pid,fd->pif/dot_general | solution.py:176
  320.5 2.5 fusion.18
  323.0 29.8 %fusion.2 = bf16[152,1024]{1,0:T(8,128)(2,1)S(1)} fusion(bf16[580,1,1024]{2,0,1:T(8,128)(2,1)} %fusion.18), kind=kCustom, calls=%all-reduce-scatter.2 | all-reduce-scatter fusion | flops 622593 | bytes 1499648
  356.3 2.9 multiply_reduce_fusion.1
  359.2 2.4 fusion.67
  364.7 6.0 %fusion.29 = f32[1024,1024]{1,0:T(8,128)} fusion(bf16[580,1024]{1,0:T(8,128)(2,1)} %get-tuple-element.103, bf16[580,1,1024]{2,1,0:T(2,128)(2,1)} %all-gather.25.cloned.1.call-done), kind=kOutput, calls=%fused_computation.52 | convolution fusion | flops 1216348160 | bytes 6569984 | tf_op jit(solution)/shard_map/pif,pid->fd/dot_general | solution.py:175
  373.2 8.7 %all-gather.6 = bf16[8,1,128]{2,1,0:T(2,128)(2,1)S(1)} all-gather(bf16[1,1,128]{2,1,0:T(2,128)(2,1)S(1)} %bitcast.197), channel_id=1, replica_groups=mesh['dp'=8,'tensor'=4] {'dp'}, dimensions={0}, use_global_device_ids=true | all-gather | bytes 2304 | tf_op jit(solution)/shard_map/all_gather | solution.py:141
  382.3 5.6 fusion.35
  389.4 3.8 fusion.17
  393.8 3.3 all-to-all-start.4
  397.1 26.1 %all-reduce.12 = (f32[1024]{0:T(1024)S(1)}, f32[1024]{0:T(1024)S(1)}, f32[4096]{0:T(1024)S(1)}, f32[1024]{0:T(1024)S(1)}) all-reduce(f32[1024]{0:T(1024)S(1)} %get-tuple-element.70, f32[1024]{0:T(1024)S(1)} %get-tuple-element.74, f32[4096]{0:T(1024)S(1)} %dynamic_update_slice.7, ...), channel_id=6, replica_groups=mesh['dp'=8,'tensor'=4] {'dp'}, use_global_device_ids=true, to_apply=%region_30.31.clone | all-reduce | flops 7168 | bytes 57344
  423.5 3.4 convolution_convert_fusion.5
  428.2 7.2 %multiply_reduce_fusion = (f32[4,580]{1,0:T(4,128)S(1)}, f32[4,580,580]{1,2,0:T(8,128)}) fusion(f32[4,580,580]{1,2,0:T(8,128)} %copy-done, f32[4,580]{1,0:T(4,128)S(1)} %log_add_fusion, bf16[580,4,64]{0,2,1:T(8,128)(2,1)S(1)} %bitcast.166, f32[580,4,64]{0,2,1:T(8,128)S(1)} %bitcast.169, f32[4,64]{1,0:T(4,128)S(1)} %add.173), kind=kOutput, calls=%fused_computation.1 | convolution fusion | flops 176568240 | bytes 11675264 | tf_op jit(solution)/shard_map/qihe,kihe->ihqk/dot_general | solution.py:217
  437.4 6.3 %multiply_convert_fusion = bf16[4,580,580]{1,2,0:T(8,128)(2,1)S(1)} fusion(f32[4,580,580]{1,2,0:T(8,128)} %get-tuple-element.117, f32[4,580,580]{1,2,0:T(8,128)} %copy-done, f32[4,580]{1,0:T(4,128)S(1)} %get-tuple-element.116, f32[4,580]{1,0:T(4,128)S(1)} %log_add_fusion), kind=kLoop, calls=%fused_computation | loop fusion | flops 5382400 | bytes 13474560 | tf_op jit(solution)/shard_map/convert_element_type | solution.py:231
  446.9 2.1 fusion.22
  449.9 3.8 fusion.19
  453.7 43.5 %fusion.64 = (bf16[152,1024]{1,0:T(8,128)(2,1)S(1)}, bf16[152,1024]{1,0:T(8,128)(2,1)S(1)}) fusion(bf16[580,1,1024]{2,0,1:T(8,128)(2,1)S(1)} %copy-done.11, bf16[580,1,1024]{2,0,1:T(8,128)(2,1)} %fusion.19), kind=kCustom, calls=%all-reduce-scatter.4 | all-reduce-scatter fusion | flops 1245185 | bytes 2998784
  497.3 3.0 collective-permute-start.3
  500.3 2.3 convolution_convert_fusion.4
  503.4 2.6 multiply_reduce_fusion.2
  506.6 3.6 all-to-all-start
  510.9 4.0 all-to-all-done
  514.8 3.3 all-to-all-start.1
  519.2 3.4 collective-permute-start.1
  522.7 4.4 all-to-all-start.3
  527.2 3.5 fusion.16
  534.3 2.8 all-to-all-done.3
  537.1 3.6 all-to-all-start.2
  540.7 2.4 fusion.66
  546.5 10.8 %all-reduce.13 = (f32[128]{0:T(128)}, f32[128]{0:T(128)}, f32[2,128]{1,0:T(2,128)}, f32[128]{0:T(128)}, f32[128]{0:T(128)}, /*index=5*/f32[128]{0:T(128)}, f32[512]{0:T(512)}, f32[128]{0:T(128)}) all-reduce(f32[128]{0:T(128)S(1)} %convert_reduce_fusion.8, ...), channel_id=1, replica_groups=mesh['dp'=8,'tensor'=4] {'tensor'}, use_global_device_ids=true, to_apply=%region_17.18 | all-reduce | flops 1536 | bytes 12288 | tf_op jit(solution)/shard_map/psum | solution.py:299
  557.4 4.3 all-to-all-done.2
  (184 shorter events, 54.0 us)
Async XLA Ops:
  7.2 27.9 %copy-start.18 = (bf16[2,128]{1,0:T(2,128)(2,1)S(1)}, bf16[2,128]{1,0:T(2,128)(2,1)}, u32[]{:S(2)}) copy-start(bf16[2,128]{1,0:T(2,128)(2,1)} %param.18) | copy-start | bytes 1540
  7.2 35.9 %copy-start.16 = (bf16[256,128]{1,0:T(8,128)(2,1)S(1)}, bf16[256,128]{1,0:T(8,128)(2,1)}, u32[]{:S(2)}) copy-start(bf16[256,128]{1,0:T(8,128)(2,1)} %param.19) | copy-start | bytes 196612
  7.2 77.5 %all-gather.15.cloned.1.call-start = ((), (), s32[]{:S(2)}) async-start(), calls=%async_computation.7 | async-start | bytes 2969600 | tf_op jit(solution)/shard_map/all_gather | solution.py:104
  31.1 0.8 copy-start.1
  33.5 77.6 %all-gather.17.cloned.1.call-start = ((), (), s32[]{:S(2)}) async-start(), calls=%async_computation.8 | async-start | bytes 1769472 | tf_op jit(solution)/shard_map/all_gather | solution.py:73
  34.2 161.4 %all-gather.21.cloned.1.call-start = ((), (), s32[]{:S(2)}) async-start(), calls=%async_computation.10 | async-start | bytes 2359296 | tf_op jit(solution)/shard_map/all_gather | solution.py:136
  35.0 198.6 %all-gather.19.cloned.1.call-start = ((), (), s32[]{:S(2)}) async-start(), calls=%async_computation.9 | async-start | bytes 2969600 | tf_op jit(solution)/shard_map/all_gather | solution.py:149
  53.0 67.7 %copy-start.10 = (bf16[256,1024]{1,0:T(8,128)(2,1)}, bf16[256,1024]{1,0:T(8,128)(2,1)S(1)}, u32[]{:S(2)}) copy-start(bf16[256,1024]{1,0:T(8,128)(2,1)S(1)} %all_gather.57) | copy-start | bytes 1572868
  115.2 1.6 copy-start.3
  116.8 2.5 copy-start
  120.6 0.7 copy-start.12
  120.6 31.7 %copy-start.19 = (bf16[128]{0:T(256)(128)(2,1)S(1)}, bf16[128]{0:T(256)(128)(2,1)}, u32[]{:S(2)}) copy-start(bf16[128]{0:T(256)(128)(2,1)} %param.20) | copy-start | bytes 772
  120.6 40.4 %copy-start.20 = (bf16[128]{0:T(256)(128)(2,1)S(1)}, bf16[128]{0:T(256)(128)(2,1)}, u32[]{:S(2)}) copy-start(bf16[128]{0:T(256)(128)(2,1)} %param.21) | copy-start | bytes 772
  120.6 48.2 %copy-start.21 = (bf16[128]{0:T(256)(128)(2,1)S(1)}, bf16[128]{0:T(256)(128)(2,1)}, u32[]{:S(2)}) copy-start(bf16[128]{0:T(256)(128)(2,1)} %param.22) | copy-start | bytes 772
  120.6 57.3 %copy-start.23 = (u32[32]{0:T(128)S(1)}, u32[32]{0:T(128)}, u32[]{:S(2)}) copy-start(u32[32]{0:T(128)} %constant.111) | copy-start | bytes 388
  121.3 58.4 %copy-start.9 = (bf16[145,1,1024]{2,0,1:T(8,128)(2,1)S(1)}, bf16[145,1,1024]{2,0,1:T(8,128)(2,1)}, u32[]{:S(2)}) copy-start(bf16[145,1,1024]{2,0,1:T(8,128)(2,1)} %param.14) | copy-start | bytes 890884
  151.0 28.2 %collective-permute-start = (bf16[21,1024]{1,0:T(8,128)(2,1)S(1)}, bf16[21,1024]{1,0:T(8,128)(2,1)S(1)}, u32[]{:S(2)}, u32[]{:S(2)}) collective-permute-start(bf16[21,1024]{1,0:T(8,128)(2,1)S(1)} %slice.26), channel_id=1, source_target_pairs={{0,1},{1,2},{2,3},{4,5},{5,6},{6,7},{8,9},{9,10},{10,11},{12,13},{... | collective-permute-start | bytes 129032
  179.7 5.6 copy-start.14
  180.8 0.8 copy-start.4
  180.8 6.8 %copy-start.17 = (bf16[512]{0:T(512)(128)(2,1)S(1)}, bf16[512]{0:T(512)(128)(2,1)}, u32[]{:S(2)}) copy-start(bf16[512]{0:T(512)(128)(2,1)} %param.24) | copy-start | bytes 3076
  185.2 99.3 %all-gather.25.cloned.1.call-start = ((), (), s32[]{:S(2)}) async-start(), calls=%async_computation.12 | async-start | bytes 2969600 | tf_op jit(solution)/shard_map/all_gather | solution.py:174
  187.0 126.3 %all-gather.23.cloned.1.call-start = ((), (), s32[]{:S(2)}) async-start(), calls=%async_computation.11 | async-start | bytes 2359296 | tf_op jit(solution)/shard_map/all_gather | solution.py:137
  187.6 236.0 %all-gather.27.cloned.1.call-start = ((), (), s32[]{:S(2)}) async-start(), calls=%async_computation.13 | async-start | bytes 2969600 | tf_op jit(solution)/shard_map/all_gather | solution.py:208
  313.3 7.1 %copy-start.24 = (bf16[1024,1024]{1,0:T(8,128)(2,1)S(1)}, bf16[1024,1024]{1,0:T(8,128)(2,1)}, u32[]{:S(2)}) copy-start(bf16[1024,1024]{1,0:T(8,128)(2,1)} %all-gather.21.cloned.1.call-done) | copy-start | bytes 6291460
  319.4 1.0 copy-start.27
  323.0 38.7 %copy-start.8 = (bf16[145,1,1024]{2,1,0:T(2,128)(2,1)S(1)}, bf16[145,1,1024]{2,1,0:T(2,128)(2,1)}, u32[]{:S(2)}) copy-start(bf16[145,1,1024]{2,1,0:T(2,128)(2,1)} %get-tuple-element.94) | copy-start | bytes 890884
  352.8 3.0 collective-permute-start.2
  362.6 0.8 copy-start.6
  364.7 198.1 %reduce-scatter.17.cloned.1.call-start = ((), (), s32[]{:S(2)}) async-start(), calls=%async_computation.15 | async-start | bytes 4718592 | tf_op jit(solution)/shard_map/reduce_scatter | solution.py:199
  370.7 2.5 copy-start.22
  370.7 11.6 %copy-start.28 = (bf16[580,1024]{1,0:T(8,128)(2,1)S(1)}, bf16[580,1024]{1,0:T(8,128)(2,1)}, u32[]{:S(2)}) copy-start(bf16[580,1024]{1,0:T(8,128)(2,1)} %copy-done.27) | copy-start | bytes 3563524
  370.7 192.1 %reduce-scatter.15.cloned.1.call-start = ((), (), s32[]{:S(2)}) async-start(), calls=%async_computation.14 | async-start | bytes 4718592 | tf_op jit(solution)/shard_map/reduce_scatter | solution.py:198
  387.8 1.6 copy-start.25
  393.8 29.7 %all-to-all-start.4 = ((bf16[8,1,128]{2,1,0:T(2,128)(2,1)}), bf16[8,1,128]{2,1,0:T(2,128)(2,1)S(1)}, u32[]{:S(2)}, u32[]{:S(2)}) async-start(bf16[8,1,128]{2,1,0:T(2,128)(2,1)} %copy.101), calls=%async_computation.4 | async-start | bytes 8192 | tf_op jit(solution)/shard_map/all_to_all | solution.py:24
  423.5 11.9 %slice-start = ((s8[5980160]{0:T(1024)(128)(4,1)}), s8[1785856]{0:T(1024)(128)(4,1)S(1)}, s32[]{:S(2)}) async-start(s8[5980160]{0:T(1024)(128)(4,1)} %bitcast.160), calls=%async_computation.16 | async-start | bytes 3571712
  428.2 7.2 %slice-start.1 = ((s8[5980160]{0:T(1024)(128)(4,1)}), s8[4194304]{0:T(1024)(128)(4,1)S(1)}, s32[]{:S(2)}) async-start(s8[5980160]{0:T(1024)(128)(4,1)} %bitcast.160), calls=%async_computation.17 | async-start | bytes 8388608
  449.1 0.7 copy-start.15
  449.8 3.8 copy-start.11
  453.7 46.6 %copy-start.13 = (bf16[4,64,580]{2,1,0:T(8,128)(2,1)S(1)}, bf16[4,64,580]{2,1,0:T(8,128)(2,1)}, u32[]{:S(2)}) copy-start(bf16[4,64,580]{2,1,0:T(8,128)(2,1)} %copy-done.12) | copy-start | bytes 890884
  497.3 6.1 %copy-start.2 = (f32[145,1,1024]{2,1,0:T(1,128)S(1)}, f32[145,1,1024]{2,1,0:T(1,128)}, u32[]{:S(2)}) copy-start(f32[145,1,1024]{2,1,0:T(1,128)} %copy-done.1) | copy-start | bytes 1781764
  497.3 5.5 collective-permute-start.3
  506.6 8.2 %all-to-all-start = ((bf16[8,1,128]{2,1,0:T(2,128)(2,1)}), bf16[8,1,128]{2,1,0:T(2,128)(2,1)S(1)}, u32[]{:S(2)}, u32[]{:S(2)}) async-start(bf16[8,1,128]{2,1,0:T(2,128)(2,1)} %copy.96), calls=%async_computation | async-start | bytes 8192 | tf_op jit(solution)/shard_map/all_to_all | solution.py:24
  514.8 7.9 %all-to-all-start.1 = ((bf16[8,1,128]{2,1,0:T(2,128)(2,1)}), bf16[8,1,128]{2,1,0:T(2,128)(2,1)S(1)}, u32[]{:S(2)}, u32[]{:S(2)}) async-start(bf16[8,1,128]{2,1,0:T(2,128)(2,1)} %copy.97), calls=%async_computation.1 | async-start | bytes 8192 | tf_op jit(solution)/shard_map/all_to_all | solution.py:24
  519.2 13.1 %collective-permute-start.1 = (bf16[21,1024]{1,0:T(8,128)(2,1)S(1)}, bf16[21,1024]{1,0:T(8,128)(2,1)S(1)}, u32[]{:S(2)}, u32[]{:S(2)}) collective-permute-start(bf16[21,1024]{1,0:T(8,128)(2,1)S(1)} %slice.27), channel_id=1, source_target_pairs={{0,1},{1,2},{2,3},{4,5},{5,6},{6,7},{8,9},{9,10},{10,11},{12,13},{... | collective-permute-start | bytes 129032
  522.7 14.4 %all-to-all-start.3 = ((bf16[8,258,128]{2,1,0:T(8,128)(2,1)}), bf16[8,258,128]{2,1,0:T(8,128)(2,1)}, u32[]{:S(2)}, u32[]{:S(2)}) async-start(bf16[8,258,128]{2,1,0:T(8,128)(2,1)} %bitcast.159), calls=%async_computation.3 | async-start | bytes 1081344 | tf_op jit(solution)/shard_map/all_to_all | solution.py:24
  530.7 2.2 copy-start.5
  534.3 8.9 %copy-start.7 = (f32[145,1,1024]{2,1,0:T(1,128)S(1)}, f32[145,1,1024]{2,1,0:T(1,128)}, u32[]{:S(2)}) copy-start(f32[145,1,1024]{2,1,0:T(1,128)} %copy-done.6) | copy-start | bytes 1781764
  537.1 24.5 %all-to-all-start.2 = ((bf16[8,3,128,256]{2,3,1,0:T(8,128)(2,1)}), bf16[8,3,128,256]{2,3,1,0:T(8,128)(2,1)S(1)}, u32[]{:S(2)}, u32[]{:S(2)}) async-start(bf16[8,3,128,256]{2,3,1,0:T(8,128)(2,1)} %bitcast.158), calls=%async_computation.2 | async-start | bytes 3145728 | tf_op jit(solution)/shard_map/all_to_all | solution.py:24
  (1 other events, 0.7 us)
Sparse Core Ops, SparseCore 0:
  33.6 51.0 all-gather.14
  86.6 24.4 all-gather.16
  113.0 27.8 all-gather.20
  185.3 48.1 all-gather.18
  235.0 49.5 all-gather.24
  286.3 26.9 all-gather.22
  364.8 49.9 all-gather.26
  418.7 50.1 reduce-scatter.16
  473.1 51.3 reduce-scatter.14
where the time goes:
time: 578 us; the launch traced here: 570 us
  blocking collectives  218 us (38%)
  waiting for transfers between devices  181 us (31%)
  matrix products  65.4 us (11%)
  other arithmetic  36.2 us (6%)
  starting transfers between devices  27.7 us (5%)
  local copies, waits for them, and re-layouts  24.6 us (4%)
  between operations  17 us (3%)
    unnamed x4, blocking collectives  128 us
    all_gather x1, waiting for transfers between devices, body(): grad_rows = lax.all_gather(masked_grad, 'tensor', axis=0, tiled=True)  41 us
    all_gather x1, waiting for transfers between devices, body(): mlp_rows = lax.all_gather(normed_two, 'tensor', axis=0, tiled=True)  37.9 us
    all_gather x1, waiting for transfers between devices, body(): attn_rows = lax.all_gather(normed_one, 'tensor', axis=0, tiled=True)  31.7 us
    all_gather x1, waiting for transfers between devices, body(): lax.all_gather(w_down, 'dp', axis=1, tiled=True)  28.8 us
    all_gather x1, waiting for transfers between devices, body(): lax.all_gather(w_qkv, 'dp', axis=1, tiled=True)  26.4 us
    all_to_all x5, starting transfers between devices, sent_and_summed(): parts = lax.all_to_all(cut_along(value, dim, size), axis, 0, 0, tiled=True)  18.2 us
    unnamed x84, local copies, waits for them, and re-layouts  14.2 us
  transfers between devices with their start and end apart: 18, of which 10 were waited for; matrix products, arithmetic and copies ran while one was open for 29% of the time, Pallas kernels for 0%

commit v1 on v0

v1 whole, which is shorter than its diff:
```python
import math

import jax
import jax.numpy as jnp
from jax import lax
from jax.experimental import pallas as pl
from jax.experimental.pallas import tpu as pltpu
from jax.sharding import PartitionSpec as P

HEAD_DIM = 64
SEQ = 577
EPS = 1e-06
NEG = -1000000000.0
MESH = pl.DeviceIdType.MESH
LANES = 128


def at_dim(dim, size):
    def view(ref, j):
        start = pl.multiple_of(j * size, size)
        index = [slice(None)] * len(ref.shape)
        index[dim] = pl.ds(start, size)
        return ref.at[tuple(index)]

    return view


def at_front(ref, j):
    return ref.at[j]


def loop(first, last, step):
    def run(k, carry):
        step(k)
        return carry

    lax.fori_loop(first, last, run, 0)


class Item:
    def __init__(self, kind, array, out_shape, src, dst):
        self.kind, self.array, self.src, self.dst = kind, array, src, dst
        self.out = jax.ShapeDtypeStruct(out_shape, array.dtype)


def whole(ref, j):
    return ref


def gather_tensor(array):
    n = lax.axis_size("tensor")
    return Item("tensor", array, (n, *array.shape), whole, at_front)


def swap_tensor(array):
    return Item("tensor", array, array.shape, at_front, at_front)


def gather_dp(array, dim):
    n = lax.axis_size("dp")
    size = array.shape[dim]
    if dim == array.ndim - 1 and size % LANES:
        return Item("gather", array, (n, *array.shape), whole, at_front)
    shape = list(array.shape)
    shape[dim] *= n
    return Item("gather", array, tuple(shape), whole, at_dim(dim, size))


def joined(value, dim):
    if value.ndim == 2:
        return value
    moved = jnp.moveaxis(value, 0, dim)
    return moved.reshape(*moved.shape[:dim], -1, *moved.shape[dim + 2 :])


def swap_dp(array, dim):
    n = lax.axis_size("dp")
    size = array.shape[dim] // n
    shape = list(array.shape)
    shape[dim] = size
    if dim == array.ndim - 1 and size % LANES:
        parts = array.reshape(*array.shape[:dim], n, size)
        parts = jnp.moveaxis(parts, dim, 0)
        return Item("swap", parts, parts.shape, at_front, at_front)
    return Item("swap", array, (n, *shape), at_dim(dim, size), at_front)


def exchange(name, number, items):
    count = len(items)
    n_t = lax.axis_size("tensor")
    n_dp = lax.axis_size("dp")
    chips = n_dp // 2
    with_tensor = any(i.kind == "tensor" for i in items)
    with_gather = any(i.kind == "gather" for i in items)
    with_swap = any(i.kind == "swap" for i in items)

    def kernel(*refs):
        srcs = refs[:count]
        dsts = refs[count : 2 * count]
        own_sem, send, recv, fsend, frecv, ssend, srecv, tsend, trecv = refs[2 * count :]
        t = lax.axis_index("tensor")
        d = lax.axis_index("dp")
        core = lax.rem(d, 2)
        chip = d // 2
        sibling = d + 1 - 2 * core
        barrier = pltpu.get_barrier_semaphore()

        def hello(dp_id, t_id):
            pl.semaphore_signal(
                barrier, inc=1, device_id=(dp_id, t_id), device_id_type=MESH
            )

        def same_core(k):
            return lax.rem(chip + k, chips) * 2 + core

        greeted = 0
        if with_tensor:
            for k in range(1, n_t):
                hello(d, lax.rem(t + k, n_t))
            greeted += n_t - 1
        if with_swap:
            loop(1, n_dp, lambda k: hello(lax.rem(d + k, n_dp), t))
            greeted += n_dp - 1
        elif with_gather:
            loop(1, chips, lambda k: hello(same_core(k), t))
            hello(sibling, t)
            greeted += chips
        pl.semaphore_wait(barrier, greeted)

        def remote(src, dst, ssem, rsem, dp_id, t_id):
            return pltpu.make_async_remote_copy(
                src_ref=src,
                dst_ref=dst,
                send_sem=ssem,
                recv_sem=rsem,
                device_id=(dp_id, t_id),
                device_id_type=MESH,
            )

        def tensor_copy(i, k, owner):
            to = lax.rem(t + k, n_t)
            return remote(
                items[i].src(srcs[i], to),
                items[i].dst(dsts[i], owner),
                tsend.at[i, k],
                trecv.at[i, k],
                d,
                to,
            )

        def swap_copy(i, k, owner):
            to = lax.rem(d + k, n_dp)
            return remote(
                items[i].src(srcs[i], to),
                items[i].dst(dsts[i], owner),
                ssend.at[i, k],
                srecv.at[i, k],
                to,
                t,
            )

        def gather_copy(i, k, owner):
            return remote(
                srcs[i],
                items[i].dst(dsts[i], owner),
                send.at[i, k],
                recv.at[i, k],
                same_core(k),
                t,
            )

        def forward_copy(i, k, owner, own):
            block = items[i].dst(dsts[i], owner)
            return remote(
                srcs[i] if own else block, block, fsend.at[i, k], frecv.at[i, k], sibling, t
            )

        def own_copy(i):
            me = t if items[i].kind == "tensor" else d
            return pltpu.make_async_copy(
                items[i].src(srcs[i], me), items[i].dst(dsts[i], me), own_sem.at[i]
            )

        def of(kind):
            return [i for i in range(count) if items[i].kind == kind]

        for k in (2, 3, 1) if n_t == 4 else range(1, n_t):
            for i in of("tensor"):
                tensor_copy(i, k, t).start()
        for i in of("gather"):
            loop(1, chips, lambda k, i=i: gather_copy(i, k, d).start())
            forward_copy(i, 0, d, True).start()
        for i in of("swap"):
            loop(1, n_dp, lambda k, i=i: swap_copy(i, k, d).start())
        for i in range(count):
            own_copy(i).start()

        def came(k):
            return lax.rem(chip + chips - k, chips) * 2

        for i in of("gather"):

            def pass_on(k, i=i):
                gather_copy(i, k, came(k) + core).wait_recv()
                forward_copy(i, k, came(k) + core, False).start()

            loop(1, chips, pass_on)
        for i in of("gather"):
            other = 1 - core
            forward_copy(i, 0, came(0) + other, True).wait_recv()
            forward_copy(i, 0, d, True).wait_send()

            def finish(k, i=i):
                forward_copy(i, k, came(k) + other, False).wait_recv()
                forward_copy(i, k, came(k) + core, False).wait_send()
                gather_copy(i, k, d).wait_send()

            loop(1, chips, finish)
        for i in of("swap"):

            def end(k, i=i):
                swap_copy(i, k, lax.rem(d + n_dp - k, n_dp)).wait_recv()
                swap_copy(i, k, d).wait_send()

            loop(1, n_dp, end)
        for i in of("tensor"):
            for k in range(1, n_t):
                tensor_copy(i, k, lax.rem(t + n_t - k, n_t)).wait_recv()
                tensor_copy(i, k, t).wait_send()
        for i in range(count):
            own_copy(i).wait()

    dma = pltpu.SemaphoreType.DMA
    sent = sum(math.prod(i.out.shape) * i.out.dtype.itemsize for i in items)
    return pl.pallas_call(
        kernel,
        out_shape=tuple(i.out for i in items),
        in_specs=[pl.BlockSpec(memory_space=pl.ANY)] * count,
        out_specs=tuple([pl.BlockSpec(memory_space=pl.ANY)] * count),
        scratch_shapes=[
            dma((count,)),
            dma((count, chips)),
            dma((count, chips)),
            dma((count, chips)),
            dma((count, chips)),
            dma((count, n_dp)),
            dma((count, n_dp)),
            dma((count, n_t)),
            dma((count, n_t)),
        ],
        compiler_params=pltpu.CompilerParams(collective_id=number, has_side_effects=True),
        cost_estimate=pl.CostEstimate(flops=0, bytes_accessed=2 * sent, transcendentals=0),
        name=name,
    )(*(i.array for i in items))


def layer_norm(values, gain, shift):
    center = values - jnp.mean(values, axis=-1, keepdims=True)
    spread = jnp.mean(center * center, axis=-1, keepdims=True)
    return center * lax.rsqrt(spread + EPS) * gain + shift


def normalized(values):
    center = values - jnp.mean(values, axis=-1, keepdims=True)
    scale = lax.rsqrt(jnp.mean(center * center, axis=-1, keepdims=True) + EPS)
    return center * scale, scale


def norm_back(grad, gain, hat, scale):
    inner = grad * gain
    mean = jnp.mean(inner, axis=-1, keepdims=True)
    along = jnp.mean(inner * hat, axis=-1, keepdims=True)
    return (inner - mean - hat * along) * scale


def exact_gelu(values):
    return jax.nn.gelu(values, approximate=False)


def summed(parts):
    return jnp.sum(parts.astype(jnp.float32), axis=0)


def body(
    tokens,
    ln1_gain,
    ln1_bias,
    w_qkv,
    b_qv,
    w_out,
    b_out,
    ln2_gain,
    ln2_bias,
    w_up,
    b_up,
    w_down,
    b_down,
    cotangent,
):
    f32, bf16 = jnp.float32, jnp.bfloat16
    slot, images, width = tokens.shape
    parts = lax.axis_size("tensor")
    n_dp = lax.axis_size("dp")
    member = lax.axis_index("tensor")
    padded = -(-slot // 16) * 16
    total = padded * parts
    row = jnp.arange(padded, dtype=jnp.int32)
    at = (jnp.arange(parts, dtype=jnp.int32)[:, None] * slot + row[None, :]).reshape(total)
    key_live = (at < SEQ) & (jnp.tile(row, parts) < slot)
    own_live = (member * slot + jnp.arange(slot, dtype=jnp.int32)) < SEQ
    scale = 1.0 / math.sqrt(HEAD_DIM)

    def widen(rows):
        return jnp.pad(rows, ((0, padded - slot), (0, 0)))

    own_tokens = widen(tokens.reshape(slot, width))
    own_grad = cotangent.reshape(slot, width)
    own_grad = widen(jnp.where(own_live[:, None], own_grad, jnp.zeros_like(own_grad)))

    small = [ln1_gain, ln1_bias, b_qv[0], b_qv[1], b_out, ln2_gain, ln2_bias, b_down, b_up]
    sizes = [s.shape[0] for s in small]
    flat = sum(sizes)
    tile = 16 * LANES
    held = -(-flat // tile) * tile

    packed = jnp.pad(jnp.concatenate(small), (0, held - flat)).reshape(-1, LANES)
    all_tokens, qkv_full, out_full, all_small = exchange(
        "gather_first",
        0,
        [
            gather_tensor(own_tokens),
            gather_dp(w_qkv, 1),
            gather_dp(w_out, 1),
            gather_dp(packed, 0),
        ],
    )
    out_full = joined(out_full, 1)
    all_small = all_small.reshape(n_dp, held).astype(f32)
    pieces, start = [], 0
    for s in sizes:
        pieces.append(all_small[:, start : start + s].reshape(-1))
        start += s
    gain_one, shift_one, q_bias, v_bias, out_bias, gain_two, shift_two, down_bias, up_bias = pieces

    local_width = qkv_full.shape[2]
    heads_here = local_width // HEAD_DIM
    head_start = member * local_width
    q_own = lax.dynamic_slice_in_dim(q_bias, head_start, local_width, 0)
    v_own = lax.dynamic_slice_in_dim(v_bias, head_start, local_width, 0)

    def split_heads(values):
        return values.reshape(total, heads_here, HEAD_DIM)

    def scores_of(query_rows, key_rows):
        raw = (
            jnp.einsum(
                "qhe,khe->hqk",
                split_heads(query_rows),
                split_heads(key_rows),
                preferred_element_type=f32,
            )
            * scale
        )
        return jnp.where(key_live[None, None, :], raw, NEG)

    hat_one, _ = normalized(all_tokens.reshape(total, width).astype(f32))
    attn_rows = (hat_one * gain_one + shift_one).astype(bf16)
    projected = jnp.einsum("pd,cde->cpe", attn_rows, qkv_full, preferred_element_type=f32)
    queries = (projected[0] + q_own).astype(bf16)
    keys = projected[1].astype(bf16)
    values = (projected[2] + v_own).astype(bf16)
    scores = scores_of(queries, keys)
    top = jnp.max(scores, axis=-1, keepdims=True)
    expo = jnp.exp(scores - top)
    denom = jnp.sum(expo, axis=-1, keepdims=True)
    probs = expo / denom
    log_total = top + jnp.log(denom)
    mixed_heads = (
        jnp.einsum(
            "hqk,khe->qhe", probs.astype(bf16), split_heads(values), preferred_element_type=f32
        )
        .reshape(total, local_width)
        .astype(bf16)
    )
    branch_part = jnp.dot(mixed_heads, out_full, preferred_element_type=f32).astype(bf16)
    branch_parts, up_full, down_full = exchange(
        "sum_branch",
        1,
        [
            swap_tensor(branch_part.reshape(parts, padded, width)),
            gather_dp(w_up, 0),
            gather_dp(w_down, 1),
        ],
    )
    down_full = joined(down_full, 1)
    inputs = own_tokens.astype(f32)
    first = inputs + (summed(branch_parts) + out_bias)
    hidden_width = up_full.shape[1]
    hidden_start = member * hidden_width
    up_own = lax.dynamic_slice_in_dim(up_bias, hidden_start, hidden_width, 0)
    hat_two, scale_two = normalized(first)
    normed_two = (hat_two * gain_two + shift_two).astype(bf16)
    mlp_rows, grad_rows = exchange(
        "gather_second", 2, [gather_tensor(normed_two), gather_tensor(own_grad)]
    )
    mlp_rows = mlp_rows.reshape(total, width)
    grad_rows = grad_rows.reshape(total, width)
    pre_act = jnp.dot(mlp_rows, up_full, preferred_element_type=f32) + up_own
    activated = exact_gelu(pre_act).astype(bf16)
    down_part = jnp.dot(activated, down_full, preferred_element_type=f32).astype(bf16)
    grad_down = jnp.einsum("pf,pd->fd", activated, grad_rows, preferred_element_type=f32)
    grad_act = jnp.einsum("pd,fd->pf", grad_rows, down_full, preferred_element_type=f32)
    gelu_pull = jax.vjp(exact_gelu, pre_act)[1]
    grad_pre = gelu_pull(grad_act)[0].astype(bf16)
    grad_up = jnp.einsum("pd,pf->df", mlp_rows, grad_pre, preferred_element_type=f32)
    up_bias_grad = lax.dynamic_update_slice_in_dim(
        jnp.zeros(up_bias.shape, f32), jnp.sum(grad_pre.astype(f32), axis=0), hidden_start, 0
    )
    two_part = jnp.einsum("pf,df->pd", grad_pre, up_full, preferred_element_type=f32).astype(bf16)
    down_parts, two_parts, up_swapped, down_swapped = exchange(
        "sum_second",
        3,
        [
            swap_tensor(down_part.reshape(parts, padded, width)),
            swap_tensor(two_part.reshape(parts, padded, width)),
            swap_dp(grad_up.astype(bf16), 0),
            swap_dp(grad_down.astype(bf16), 1),
        ],
    )
    mixed = (first + summed(down_parts) + down_bias).astype(bf16)
    up_w_sum = summed(up_swapped)
    down_w_sum = summed(down_swapped)
    grad_normed_two = summed(two_parts)
    masked_float = own_grad.astype(f32)
    grad_first = masked_float + norm_back(grad_normed_two, gain_two, hat_two, scale_two)
    grad_gain_two = jnp.sum(grad_normed_two * hat_two, axis=0)
    grad_shift_two = jnp.sum(grad_normed_two, axis=0)
    grad_down_bias = jnp.sum(masked_float, axis=0)
    grad_branch = grad_first.astype(bf16)
    grad_out_bias = jnp.sum(grad_branch.astype(f32), axis=0)
    (branch_rows,) = exchange("gather_third", 4, [gather_tensor(grad_branch)])
    branch_rows = branch_rows.reshape(total, width)
    grad_out_w = jnp.einsum("pe,pd->ed", mixed_heads, branch_rows, preferred_element_type=f32)
    grad_heads = jnp.einsum("pd,ed->pe", branch_rows, out_full, preferred_element_type=f32).astype(
        bf16
    )
    grad_split = split_heads(grad_heads)
    probs_again = jnp.exp(scores_of(queries, keys) - log_total)
    grad_probs = jnp.einsum(
        "qhe,khe->hqk", grad_split, split_heads(values), preferred_element_type=f32
    )
    grad_values = (
        jnp.einsum("hqk,qhe->khe", probs_again.astype(bf16), grad_split, preferred_element_type=f32)
        .reshape(total, local_width)
        .astype(bf16)
    )
    inner = jnp.sum(probs_again * grad_probs, axis=-1, keepdims=True)
    grad_scores = (probs_again * (grad_probs - inner)).astype(bf16)
    grad_queries = (
        (
            jnp.einsum("hqk,khe->qhe", grad_scores, split_heads(keys), preferred_element_type=f32)
            * scale
        )
        .reshape(total, local_width)
        .astype(bf16)
    )
    grad_keys = (
        (
            jnp.einsum(
                "hqk,qhe->khe", grad_scores, split_heads(queries), preferred_element_type=f32
            )
            * scale
        )
        .reshape(total, local_width)
        .astype(bf16)
    )
    grad_qkv = jnp.stack([grad_queries, grad_keys, grad_values])
    grad_qkv_w = jnp.einsum("pd,cpe->cde", attn_rows, grad_qkv, preferred_element_type=f32)

    def own_columns(values):
        return lax.dynamic_update_slice_in_dim(
            jnp.zeros((local_width * parts,), f32),
            jnp.sum(values.astype(f32), axis=0),
            head_start,
            0,
        )

    one_part = jnp.einsum("cpe,cde->pd", grad_qkv, qkv_full, preferred_element_type=f32)
    grad_gain_one = jnp.sum(one_part * hat_one, axis=0)
    grad_shift_one = jnp.sum(one_part, axis=0)
    small_grads = [
        grad_gain_one,
        grad_shift_one,
        own_columns(grad_queries),
        own_columns(grad_values),
        grad_out_bias,
        grad_gain_two,
        grad_shift_two,
        grad_down_bias,
        up_bias_grad,
    ]
    packed_grads = jnp.concatenate([g.reshape(n_dp, -1) for g in small_grads], axis=1)
    packed_grads = jnp.pad(packed_grads, ((0, 0), (0, held - flat))).reshape(-1, LANES)
    one_parts, qkv_swapped, out_swapped, small_swapped = exchange(
        "sum_third",
        5,
        [
            swap_tensor(one_part.astype(bf16).reshape(parts, padded, width)),
            swap_dp(grad_qkv_w.astype(bf16), 1),
            swap_dp(grad_out_w.astype(bf16), 1),
            swap_dp(packed_grads, 0),
        ],
    )
    (small_all,) = exchange("sum_small", 6, [gather_tensor(summed(small_swapped))])
    hat_own, scale_own = normalized(inputs)
    grad_tokens = grad_first + norm_back(summed(one_parts), gain_one, hat_own, scale_own)
    small_sum = summed(small_all).reshape(held)
    done, start = [], 0
    for s in sizes:
        done.append(small_sum[start : start + s])
        start += s
    return (
        mixed[:slot].reshape(slot, images, width),
        grad_tokens[:slot].reshape(slot, images, width),
        done[0],
        done[1],
        summed(qkv_swapped),
        jnp.stack([done[2], done[3]]),
        summed(out_swapped),
        done[4],
        done[5],
        done[6],
        summed(up_swapped),
        done[8],
        down_w_sum,
        done[7],
    )


def solution(mesh):
    placed = (
        P("tensor", "dp", None),
        P("dp"),
        P("dp"),
        P(None, "dp", "tensor"),
        P(None, "dp"),
        P("tensor", "dp"),
        P("dp"),
        P("dp"),
        P("dp"),
        P("dp", "tensor"),
        P("dp"),
        P("tensor", "dp"),
        P("dp"),
        P("tensor", "dp", None),
    )
    return jax.shard_map(
        body,
        mesh=mesh,
        in_specs=placed,
        out_specs=(
            P("tensor", "dp", None),
            P("tensor", "dp", None),
            P("dp"),
            P("dp"),
            P(None, "dp", "tensor"),
            P(None, "dp"),
            P("tensor", "dp"),
            P("dp"),
            P("dp"),
            P("dp"),
            P("dp", "tensor"),
            P("dp"),
            P("tensor", "dp"),
            P("dp"),
        ),
        check_vma=False,
    )
```

time: 578 us -> 375 us (0.65)
  Pallas kernels: 0 us -> 259 us
  blocking collectives: 218 us -> 0 us
  waiting for transfers between devices: 181 us -> 0 us
  starting transfers between devices: 27.7 us -> 0 us
  between operations: 17 us -> 1.69 us
  other arithmetic: 36.2 us -> 24.8 us
  matrix products: 65.4 us -> 59.1 us
    pallas_call x0 -> x7, Pallas kernels: none -> 259 us  [exchange(): pl.pallas_call(kernel, out_shape=tuple((i.out for i in items)), in_specs=...]
    all_gather x7 -> x0, waiting for transfers between devices: 166 us -> none  [the longest x1 41 us: body(): grad_rows = lax.all_gather(masked_grad, 'tensor', axis=0, tiled=True)]
    unnamed x4 -> x0, blocking collectives: 128 us -> none
    all_gather x9 -> x0, blocking collectives: 78.9 us -> none  [the longest x1 10.3 us: body(): lax.all_gather(ln1_gain, 'dp', axis=0, tiled=True)]
    all_to_all x5 -> x0, starting transfers between devices: 18.2 us -> none  [sent_and_summed(): parts = lax.all_to_all(cut_along(value, dim, size), axis, 0, 0, tiled=True)]
    all_to_all x5 -> x0, waiting for transfers between devices: 11.2 us -> none  [sent_and_summed(): parts = lax.all_to_all(cut_along(value, dim, size), axis, 0, 0, tiled=True)]
    psum x1 -> x0, blocking collectives: 10.8 us -> none  [body(): lax.psum((gain_one_sum, shift_one_sum, qv_b_sum, out_b_sum, gain_two_sum,...]
    unnamed x4 -> x0, starting transfers between devices: 9.16 us -> none
  transfers between devices with their start and end apart: 18 -> 0, of which waited for: 10 -> 0; matrix products, arithmetic and copies ran while one was open for 29% -> 0% of each run, Pallas kernels for 0% -> 0%
where the time goes in v1:
time: 375 us; the launch traced here: 368 us
  Pallas kernels  259 us (69%)
  matrix products  59.1 us (16%)
  other arithmetic  24.8 us (7%)
  local copies, waits for them, and re-layouts  23.3 us (6%)
    pallas_call x7, Pallas kernels, exchange(): pl.pallas_call(kernel, out_shape=tuple((i.out for i in items)), in_specs=...  259 us
    reduce_sum x9, other arithmetic, summed(): return jnp.sum(parts.astype(jnp.float32), axis=0)  11.9 us
    unnamed x83, local copies, waits for them, and re-layouts  11.4 us
    dot_general x1, matrix products, body(): jnp.einsum('pd,fd->pf', grad_rows, down_full, preferred_element_type=f32)  9.78 us

profile of v1, /device:TPU:0, one launch (start us, length us, event | category | flops | bytes accessed | tf_op | source)
XLA Modules:
  0.0 367.7 jit_solution(10518912038389569144)
XLA Ops:
  0.6 1.7 pad.15.refs_0_
  3.2 0.8 dynamic-update-slice.10
  5.2 0.8 dynamic-update-slice.13
  6.0 0.8 dynamic-update-slice.14
  7.7 0.8 dynamic-update-slice.16
  9.8 30.9 %gather_first.1 = (bf16[4,160,1024]{2,1,0:T(8,128)(2,1)}, bf16[3,1024,256]{2,1,0:T(8,128)(2,1)}, bf16[256,1024]{1,0:T(8,128)(2,1)}, bf16[128,128]{1,0:T(8,128)(2,1)}) custom-call(bf16[160,1024]{1,0:T(8,128)(2,1)} %pad.15.refs_0_, bf16[3,128,256]{2,1,0:T(8,128)(2,1)} %refs_1_.2, bf16[256,128]{1,0:T(8,128)(2,1)} %refs_2_.2, ...), custom_call_target="tpu_custom_call" | custom-call | bytes 6881280 | tf_op jit(solution)/shard_map/gather_first/pallas_call | solution.py:235
  40.7 0.9 reshape.341
  41.6 1.6 convert_reduce_fusion.9
  43.2 1.8 multiply_reduce_fusion.1
  45.7 3.3 convolution_bitcast_fusion
  49.6 1.6 fusion.42
  51.2 0.9 fusion
  52.1 1.8 copy-done
  54.1 4.2 %fusion.22 = bf16[4,64,640]{2,1,0:T(8,128)(2,1)S(1)} fusion(f32[4,640,640]{1,2,0:T(8,128)} %copy-done, f32[4,640]{1,0:T(4,128)S(1)} %fusion, f32[4,640]{1,0:T(4,128)S(1)} %get-tuple-element.101, f32[640,4,64]{0,2,1:T(8,128)S(1)} %bitcast.150, f32[4,64]{1,0:T(4,128)S(1)} %add.171), kind=kOutput, calls=%fused_computation.63 | convolution fusion | flops 215121920 | bytes 7558144 | tf_op jit(solution)/shard_map/hqk,khe->qhe/dot_general | solution.py:379
  58.3 1.6 convolution_convert_fusion.3
  59.9 34.5 %sum_branch.1 = (bf16[4,160,1024]{2,1,0:T(8,128)(2,1)}, bf16[1024,1024]{1,0:T(8,128)(2,1)}, bf16[1024,1024]{1,0:T(8,128)(2,1)}) custom-call(bf16[4,160,1024]{2,1,0:T(8,128)(2,1)} %bitcast.143, bf16[128,1024]{1,0:T(8,128)(2,1)} %refs_1_.3, bf16[1024,128]{1,0:T(8,128)(2,1)} %refs_2_.3), custom_call_target="tpu_custom_call" | custom-call | bytes 11010048 | tf_op jit(solution)/shard_map/sum_branch/pallas_call | solution.py:235
  94.4 1.7 convert_reduce_fusion.8
  96.7 0.9 add_convert_fusion.2.refs_0_
  98.5 50.3 %gather_second.1 = (bf16[4,160,1024]{2,1,0:T(8,128)(2,1)}, bf16[4,160,1024]{2,1,0:T(8,128)(2,1)}) custom-call(bf16[160,1024]{1,0:T(8,128)(2,1)} %add_convert_fusion.2.refs_0_, bf16[160,1024]{1,0:T(8,128)(2,1)} %pad.17.refs_1_), custom_call_target="tpu_custom_call" | custom-call | bytes 5242880 | tf_op jit(solution)/shard_map/gather_second/pallas_call | solution.py:235
  148.8 5.1 %fusion.43 = f32[640,1024]{1,0:T(8,128)} fusion(bf16[640,1024]{1,0:T(8,128)(2,1)} %bitcast.168, bf16[1024,1024]{1,0:T(8,128)(2,1)} %get-tuple-element.37), kind=kOutput, calls=%fused_computation.153 | convolution fusion | flops 1342177280 | bytes 6029312 | tf_op jit(solution)/shard_map/dot_general | solution.py:408
  154.0 9.8 %convert_reduce_fusion.6 = (f32[1024]{0:T(1024)S(1)}, bf16[640,1024]{1,0:T(8,128)(2,1)S(1)}, f32[640,1024]{1,0:T(8,128)S(1)}) fusion(f32[640,1024]{1,0:T(8,128)} %fusion.43, f32[1024]{0:T(1024)S(1)} %dynamic_slice.11, bf16[640,1024]{1,0:T(8,128)(2,1)} %bitcast.166, bf16[1024,1024]{1,0:T(8,128)(2,1)} %get-tuple-element.38), kind=kOutput, calls=%fused_computation.25 | convolution fusion | flops 1391328256 | bytes 9969664 | tf_op jit(solution)/shard_map/pd,fd->pf/dot_general | solution.py:412
  164.5 0.9 copy-done.26
  165.3 2.6 convolution_convert_fusion.5
  168.0 2.6 convolution_convert_fusion.4
  170.6 3.2 convolution_convert_fusion.1.refs_2_
  173.8 3.2 convolution_convert_fusion.refs_3_
  177.0 60.0 %sum_second.1 = (bf16[4,160,1024]{2,1,0:T(8,128)(2,1)}, bf16[4,160,1024]{2,1,0:T(8,128)(2,1)}, bf16[8,128,1024]{2,1,0:T(8,128)(2,1)}, bf16[8,1024,128]{2,1,0:T(8,128)(2,1)}) custom-call(bf16[4,160,1024]{2,1,0:T(8,128)(2,1)} %bitcast.156, bf16[4,160,1024]{2,1,0:T(8,128)(2,1)} %bitcast.157, bf16[1024,1024]{1,0:T(8,128)(2,1)} %convolution_convert_fusion.1.refs_2_, ...), custom_call_target="tpu_custom_call" | custom-call | bytes 13631488 | tf_op jit(solution)/shard_map/sum_second/pallas_call | solution.py:235
  237.1 1.7 convert_reduce_fusion.7
  240.5 1.3 convert_reduce_fusion.13
  241.8 39.1 %gather_third.1 = bf16[4,160,1024]{2,1,0:T(8,128)(2,1)} custom-call(bf16[160,1024]{1,0:T(8,128)(2,1)} %get-tuple-element.76.refs_0_), custom_call_target="tpu_custom_call" | custom-call | bytes 2621440 | tf_op jit(solution)/shard_map/gather_third/pallas_call | solution.py:235
  280.9 1.9 convolution_convert_fusion.7
  282.8 4.9 %convert_reduce_fusion.14 = (f32[4,64]{1,0:T(4,128)S(1)}, bf16[4,64,640]{2,1,0:T(8,128)(2,1)}) fusion(bf16[640,4,64]{0,2,1:T(8,128)(2,1)S(1)} %bitcast.152, f32[4,640,640]{1,2,0:T(8,128)} %copy-done, f32[4,640]{1,0:T(4,128)S(1)} %log_add_fusion), kind=kOutput, calls=%fused_computation.78 | convolution fusion | flops 213483264 | bytes 7220224 | tf_op jit(solution)/shard_map/hqk,qhe->khe/dot_general | solution.py:453
  287.8 2.0 copy.35
  289.8 4.8 %multiply_reduce_fusion = (f32[4,640]{1,0:T(4,128)S(1)}, f32[4,640,640]{1,2,0:T(8,128)S(1)}) fusion(f32[4,640,640]{1,2,0:T(8,128)} %copy-done, f32[4,640]{1,0:T(4,128)S(1)} %log_add_fusion, bf16[640,4,64]{0,2,1:T(8,128)(2,1)} %bitcast.153, f32[640,4,64]{0,2,1:T(8,128)} %bitcast.151, f32[4,64]{1,0:T(4,128)S(1)} %add.171), kind=kOutput, calls=%fused_computation.1 | convolution fusion | flops 214955520 | bytes 14111744 | tf_op jit(solution)/shard_map/qhe,khe->hqk/dot_general | solution.py:449
  294.6 1.6 multiply_convert_fusion
  296.2 1.7 copy-done.1
  297.9 1.2 fusion.18
  299.3 2.8 convert_reduce_fusion.15
  302.3 2.3 bitcast_convert_fusion
  304.6 2.6 fusion.14.refs_1_
  307.2 1.4 convolution_convert_fusion.6.refs_2_
  311.0 32.6 %sum_third.1 = (bf16[4,160,1024]{2,1,0:T(8,128)(2,1)}, bf16[8,3,128,256]{3,2,1,0:T(8,128)(2,1)}, bf16[8,256,128]{2,1,0:T(8,128)(2,1)}, f32[8,16,128]{2,1,0:T(8,128)}) custom-call(bf16[4,160,1024]{2,1,0:T(8,128)(2,1)} %bitcast.155, bf16[3,1024,256]{2,1,0:T(8,128)(2,1)} %fusion.14.refs_1_, bf16[256,1024]{1,0:T(8,128)(2,1)} %convolution_convert_fusion.6.refs_2_, ...), custom_call_target="tpu_custom_call" | custom-call | bytes 6946816 | tf_op jit(solution)/shard_map/sum_third/pallas_call | solution.py:235
  343.7 1.7 convert_reduce_fusion.5
  345.9 1.4 copy.38
  347.9 11.4 %sum_small.1 = f32[4,16,128]{2,1,0:T(8,128)} custom-call(f32[16,128]{1,0:T(8,128)} %reduce_sum.310.refs_0_), custom_call_target="tpu_custom_call" | custom-call | bytes 65536 | tf_op jit(solution)/shard_map/sum_small/pallas_call | solution.py:235
  360.6 2.5 convert_reduce_fusion.4
  364.5 1.1 convert_reduce_fusion.1
  366.2 1.1 convert_reduce_fusion
  (137 shorter events, 16.4 us)
Async XLA Ops:
  40.7 4.5 %copy-start.2 = (bf16[4,160,1024]{2,1,0:T(8,128)(2,1)S(1)}, bf16[4,160,1024]{2,1,0:T(8,128)(2,1)}, u32[]{:S(2)}) copy-start(bf16[4,160,1024]{2,1,0:T(8,128)(2,1)} %get-tuple-element.32) | copy-start | bytes 3932164
  45.7 3.3 copy-start.14
  49.1 2.1 copy-start.6
  49.2 9.1 %copy-start.8 = (f32[1,640,256]{1,2,0:T(8,128)}, f32[1,640,256]{1,2,0:T(8,128)S(1)}, u32[]{:S(2)}) copy-start(f32[1,640,256]{1,2,0:T(8,128)S(1)} %get-tuple-element.80) | copy-start | bytes 1966084
  51.2 2.7 copy-start
  54.1 4.2 %copy-start.20 = (bf16[256,1024]{1,0:T(8,128)(2,1)S(1)}, bf16[256,1024]{1,0:T(8,128)(2,1)}, u32[]{:S(2)}) copy-start(bf16[256,1024]{1,0:T(8,128)(2,1)} %get-tuple-element.34) | copy-start | bytes 1572868
  58.3 36.1 %copy-start.17 = (bf16[4,64,640]{2,1,0:T(8,128)(2,1)}, bf16[4,64,640]{2,1,0:T(8,128)(2,1)S(1)}, u32[]{:S(2)}) copy-start(bf16[4,64,640]{2,1,0:T(8,128)(2,1)S(1)} %fusion.22) | copy-start | bytes 983044
  58.3 37.8 %copy-start.5 = (bf16[145,1,1024]{2,0,1:T(8,128)(2,1)S(1)}, bf16[145,1,1024]{2,0,1:T(8,128)(2,1)}, u32[]{:S(2)}) copy-start(bf16[145,1,1024]{2,0,1:T(8,128)(2,1)} %param.14) | copy-start | bytes 890884
  94.4 3.3 copy-start.23
  153.9 9.8 %copy-start.9 = (f32[640,1024]{1,0:T(8,128)S(1)}, f32[640,1024]{1,0:T(8,128)}, u32[]{:S(2)}) copy-start(f32[640,1024]{1,0:T(8,128)} %fusion.43) | copy-start | bytes 7864324
  163.7 1.6 copy-start.26
  165.3 2.6 copy-start.25
  168.0 2.6 copy-start.29
  170.6 3.2 copy-start.28
  237.1 2.5 copy-start.16
  240.1 40.8 %copy-start.21 = (bf16[256,1024]{1,0:T(8,128)(2,1)S(1)}, bf16[256,1024]{1,0:T(8,128)(2,1)}, u32[]{:S(2)}) copy-start(bf16[256,1024]{1,0:T(8,128)(2,1)} %get-tuple-element.34) | copy-start | bytes 1572868
  282.8 4.9 %copy-start.13 = (bf16[640,256]{0,1:T(8,128)(2,1)}, bf16[640,256]{0,1:T(8,128)(2,1)S(1)}, u32[]{:S(2)}) copy-start(bf16[640,256]{0,1:T(8,128)(2,1)S(1)} %convolution_convert_fusion.7) | copy-start | bytes 983044
  287.8 6.9 %slice-start = ((s8[6553600]{0:T(1024)(128)(4,1)}), s8[2359296]{0:T(1024)(128)(4,1)S(1)}, s32[]{:S(2)}) async-start(s8[6553600]{0:T(1024)(128)(4,1)} %bitcast.137), calls=%async_computation | async-start | bytes 4718592
  289.8 4.8 %slice-start.1 = ((s8[6553600]{0:T(1024)(128)(4,1)}), s8[4194304]{0:T(1024)(128)(4,1)S(1)}, s32[]{:S(2)}) async-start(s8[6553600]{0:T(1024)(128)(4,1)} %bitcast.137), calls=%async_computation.1 | async-start | bytes 8388608
  296.2 1.7 copy-start.1
  297.9 1.4 copy-start.7
  299.1 3.2 copy-start.22
  299.1 3.2 copy-start.27
  302.3 2.3 copy-start.15
  304.6 2.6 copy-start.4
  304.6 2.6 copy-start.18
  307.2 1.4 copy-start.3
  343.6 2.0 copy-start.10
  345.4 2.0 copy-start.24
  345.7 18.1 %copy-start.19 = (bf16[8,256,128]{2,1,0:T(8,128)(2,1)S(1)}, bf16[8,256,128]{2,1,0:T(8,128)(2,1)}, u32[]{:S(2)}) copy-start(bf16[8,256,128]{2,1,0:T(8,128)(2,1)} %get-tuple-element.45) | copy-start | bytes 1572868
  345.9 18.6 %copy-start.12 = (bf16[8,128,1024]{2,1,0:T(8,128)(2,1)S(1)}, bf16[8,128,1024]{2,1,0:T(8,128)(2,1)}, u32[]{:S(2)}) copy-start(bf16[8,128,1024]{2,1,0:T(8,128)(2,1)} %get-tuple-element.46) | copy-start | bytes 6291460
  360.6 5.6 %copy-start.11 = (bf16[8,1024,128]{2,1,0:T(8,128)(2,1)S(1)}, bf16[8,1024,128]{2,1,0:T(8,128)(2,1)}, u32[]{:S(2)}) copy-start(bf16[8,1024,128]{2,1,0:T(8,128)(2,1)} %get-tuple-element.47) | copy-start | bytes 6291460

commit v2 on v1

--- a/solution.py
+++ b/solution.py
@@ -38,8 +38,9 @@
 
 
 class Item:
-    def __init__(self, kind, array, out_shape, src, dst):
+    def __init__(self, kind, array, out_shape, src, dst, turned=False):
         self.kind, self.array, self.src, self.dst = kind, array, src, dst
+        self.turned = turned
         self.out = jax.ShapeDtypeStruct(out_shape, array.dtype)
 
 
@@ -47,13 +48,18 @@
     return ref
 
 
-def gather_tensor(array):
+def gather_tensor(array, turned=False):
     n = lax.axis_size("tensor")
-    return Item("tensor", array, (n, *array.shape), whole, at_front)
-
-
-def swap_tensor(array):
-    return Item("tensor", array, array.shape, at_front, at_front)
+    return Item("tensor", array, (n, *array.shape), whole, at_front, turned)
+
+
+def swap_tensor(array, turned=False):
+    return Item("tensor", array, array.shape, at_front, at_front, turned)
+
+
+def permuted(block, k):
+    n = lax.axis_size("tensor")
+    return lax.ppermute(block, "tensor", [(j, (j + k) % n) for j in range(n)])
 
 
 def gather_dp(array, dim):
@@ -85,19 +91,23 @@
     return Item("swap", array, (n, *shape), at_dim(dim, size), at_front)
 
 
-def exchange(name, number, items):
+def exchange(name, number, items, small=None):
     count = len(items)
+    extra = 0 if small is None else 1
     n_t = lax.axis_size("tensor")
     n_dp = lax.axis_size("dp")
     chips = n_dp // 2
     with_tensor = any(i.kind == "tensor" for i in items)
     with_gather = any(i.kind == "gather" for i in items)
     with_swap = any(i.kind == "swap" for i in items)
+    if extra:
+        small_rows = small.shape[0] // n_dp
 
     def kernel(*refs):
         srcs = refs[:count]
-        dsts = refs[count : 2 * count]
-        own_sem, send, recv, fsend, frecv, ssend, srecv, tsend, trecv = refs[2 * count :]
+        dsts = refs[count + extra : 2 * count + extra]
+        scratch = refs[2 * (count + extra) :]
+        own_sem, send, recv, fsend, frecv, ssend, srecv, tsend, trecv = scratch[:9]
         t = lax.axis_index("tensor")
         d = lax.axis_index("dp")
         core = lax.rem(d, 2)
@@ -139,9 +149,10 @@
 
         def tensor_copy(i, k, owner):
             to = lax.rem(t + k, n_t)
+            turned = items[i].turned
             return remote(
-                items[i].src(srcs[i], to),
-                items[i].dst(dsts[i], owner),
+                items[i].src(srcs[i], (n_t - k) % n_t if turned else to),
+                items[i].dst(dsts[i], k if turned else owner),
                 tsend.at[i, k],
                 trecv.at[i, k],
                 d,
@@ -177,9 +188,29 @@
 
         def own_copy(i):
             me = t if items[i].kind == "tensor" else d
+            me = 0 if items[i].turned else me
             return pltpu.make_async_copy(
                 items[i].src(srcs[i], me), items[i].dst(dsts[i], me), own_sem.at[i]
             )
+
+        if extra:
+            small_in, small_out = refs[count], refs[2 * count + 1]
+            small_got, small_sum, dsend, drecv, esend, erecv = scratch[9:]
+            view = at_dim(0, small_rows)
+
+            def small_swap(k, owner):
+                to = lax.rem(d + k, n_dp)
+                return remote(
+                    view(small_in, to), small_got.at[owner], dsend.at[k], drecv.at[k], to, t
+                )
+
+            def small_gather(k, owner):
+                to = lax.rem(t + k, n_t)
+                return remote(
+                    small_sum, small_out.at[owner], esend.at[k], erecv.at[k], d, to
+                )
+
+            loop(1, n_dp, lambda k: small_swap(k, d).start())
 
         def of(kind):
             return [i for i in range(count) if items[i].kind == kind]
@@ -194,6 +225,13 @@
             loop(1, n_dp, lambda k, i=i: swap_copy(i, k, d).start())
         for i in range(count):
             own_copy(i).start()
+        if extra:
+            small_got[d] = small_in[pl.ds(pl.multiple_of(d * small_rows, small_rows), small_rows)]
+            loop(1, n_dp, lambda k: small_swap(k, lax.rem(d + n_dp - k, n_dp)).wait_recv())
+            small_sum[...] = jnp.sum(small_got[...], axis=0)
+            for k in range(1, n_t):
+                small_gather(k, t).start()
+            small_out[t] = small_sum[...]
 
         def came(k):
             return lax.rem(chip + chips - k, chips) * 2
@@ -229,14 +267,37 @@
                 tensor_copy(i, k, t).wait_send()
         for i in range(count):
             own_copy(i).wait()
+        if extra:
+            loop(1, n_dp, lambda k: small_swap(k, d).wait_send())
+            for k in range(1, n_t):
+                small_gather(k, lax.rem(t + n_t - k, n_t)).wait_recv()
+                small_gather(k, t).wait_send()
 
     dma = pltpu.SemaphoreType.DMA
     sent = sum(math.prod(i.out.shape) * i.out.dtype.itemsize for i in items)
+    shapes = [i.out for i in items]
+    specs = [pl.BlockSpec(memory_space=pl.ANY)] * count
+    own_scratch = []
+    arrays = [i.array for i in items]
+    if extra:
+        assert with_tensor and with_swap
+        arrays.append(small)
+        block = (small_rows, small.shape[1])
+        shapes.append(jax.ShapeDtypeStruct((n_t, *block), small.dtype))
+        specs.append(pl.BlockSpec(memory_space=pltpu.VMEM))
+        own_scratch = [
+            pltpu.VMEM((n_dp, *block), small.dtype),
+            pltpu.VMEM(block, small.dtype),
+            dma((n_dp,)),
+            dma((n_dp,)),
+            dma((n_t,)),
+            dma((n_t,)),
+        ]
     return pl.pallas_call(
         kernel,
-        out_shape=tuple(i.out for i in items),
-        in_specs=[pl.BlockSpec(memory_space=pl.ANY)] * count,
-        out_specs=tuple([pl.BlockSpec(memory_space=pl.ANY)] * count),
+        out_shape=tuple(shapes),
+        in_specs=specs,
+        out_specs=tuple(specs),
         scratch_shapes=[
             dma((count,)),
             dma((count, chips)),
@@ -247,11 +308,21 @@
             dma((count, n_dp)),
             dma((count, n_t)),
             dma((count, n_t)),
+            *own_scratch,
         ],
         compiler_params=pltpu.CompilerParams(collective_id=number, has_side_effects=True),
         cost_estimate=pl.CostEstimate(flops=0, bytes_accessed=2 * sent, transcendentals=0),
         name=name,
-    )(*(i.array for i in items))
+    )(*arrays)
+
+
+def side_by_side(pieces, sizes, held):
+    placed, start = 0, 0
+    for piece, size in zip(pieces, sizes):
+        around = [(0, 0)] * (piece.ndim - 1) + [(start, held - start - size)]
+        placed = placed + jnp.pad(piece, around)
+        start += size
+    return placed
 
 
 def layer_norm(values, gain, shift):
@@ -323,7 +394,7 @@
     tile = 16 * LANES
     held = -(-flat // tile) * tile
 
-    packed = jnp.pad(jnp.concatenate(small), (0, held - flat)).reshape(-1, LANES)
+    packed = side_by_side(small, sizes, held).reshape(-1, LANES)
     all_tokens, qkv_full, out_full, all_small = exchange(
         "gather_first",
         0,
@@ -335,6 +406,8 @@
         ],
     )
     out_full = joined(out_full, 1)
+    all_tokens, own_grad = lax.optimization_barrier((all_tokens, own_grad))
+    grad_blocks = [permuted(own_grad, k) for k in range(1, parts)]
     all_small = all_small.reshape(n_dp, held).astype(f32)
     pieces, start = [], 0
     for s in sizes:
@@ -383,6 +456,8 @@
         .astype(bf16)
     )
     branch_part = jnp.dot(mixed_heads, out_full, preferred_element_type=f32).astype(bf16)
+    branch_part, grad_blocks = lax.optimization_barrier((branch_part, grad_blocks))
+    grad_rows = jnp.concatenate([own_grad, *grad_blocks])
     branch_parts, up_full, down_full = exchange(
         "sum_branch",
         1,
@@ -400,11 +475,8 @@
     up_own = lax.dynamic_slice_in_dim(up_bias, hidden_start, hidden_width, 0)
     hat_two, scale_two = normalized(first)
     normed_two = (hat_two * gain_two + shift_two).astype(bf16)
-    mlp_rows, grad_rows = exchange(
-        "gather_second", 2, [gather_tensor(normed_two), gather_tensor(own_grad)]
-    )
+    (mlp_rows,) = exchange("gather_second", 2, [gather_tensor(normed_two, turned=True)])
     mlp_rows = mlp_rows.reshape(total, width)
-    grad_rows = grad_rows.reshape(total, width)
     pre_act = jnp.dot(mlp_rows, up_full, preferred_element_type=f32) + up_own
     activated = exact_gelu(pre_act).astype(bf16)
     down_part = jnp.dot(activated, down_full, preferred_element_type=f32).astype(bf16)
@@ -417,19 +489,14 @@
         jnp.zeros(up_bias.shape, f32), jnp.sum(grad_pre.astype(f32), axis=0), hidden_start, 0
     )
     two_part = jnp.einsum("pf,df->pd", grad_pre, up_full, preferred_element_type=f32).astype(bf16)
-    down_parts, two_parts, up_swapped, down_swapped = exchange(
+    two_parts, up_swapped = exchange(
         "sum_second",
         3,
         [
-            swap_tensor(down_part.reshape(parts, padded, width)),
-            swap_tensor(two_part.reshape(parts, padded, width)),
+            swap_tensor(two_part.reshape(parts, padded, width), turned=True),
             swap_dp(grad_up.astype(bf16), 0),
-            swap_dp(grad_down.astype(bf16), 1),
         ],
     )
-    mixed = (first + summed(down_parts) + down_bias).astype(bf16)
-    up_w_sum = summed(up_swapped)
-    down_w_sum = summed(down_swapped)
     grad_normed_two = summed(two_parts)
     masked_float = own_grad.astype(f32)
     grad_first = masked_float + norm_back(grad_normed_two, gain_two, hat_two, scale_two)
@@ -438,7 +505,12 @@
     grad_down_bias = jnp.sum(masked_float, axis=0)
     grad_branch = grad_first.astype(bf16)
     grad_out_bias = jnp.sum(grad_branch.astype(f32), axis=0)
-    (branch_rows,) = exchange("gather_third", 4, [gather_tensor(grad_branch)])
+    branch_rows, down_swapped = exchange(
+        "gather_third", 4, [gather_tensor(grad_branch), swap_dp(grad_down.astype(bf16), 1)]
+    )
+    branch_rows, down_part = lax.optimization_barrier((branch_rows, down_part))
+    down_blocks = down_part.reshape(parts, padded, width)
+    down_parts = [permuted(down_blocks[parts - k], k) for k in (1, parts - 1)]
     branch_rows = branch_rows.reshape(total, width)
     grad_out_w = jnp.einsum("pe,pd->ed", mixed_heads, branch_rows, preferred_element_type=f32)
     grad_heads = jnp.einsum("pd,ed->pe", branch_rows, out_full, preferred_element_type=f32).astype(
@@ -455,6 +527,8 @@
         .astype(bf16)
     )
     inner = jnp.sum(probs_again * grad_probs, axis=-1, keepdims=True)
+    inner, down_parts, down_blocks = lax.optimization_barrier((inner, down_parts, down_blocks))
+    down_parts += [permuted(down_blocks[parts - k], k) for k in range(2, parts - 1)]
     grad_scores = (probs_again * (grad_probs - inner)).astype(bf16)
     grad_queries = (
         (
@@ -499,19 +573,23 @@
         grad_down_bias,
         up_bias_grad,
     ]
-    packed_grads = jnp.concatenate([g.reshape(n_dp, -1) for g in small_grads], axis=1)
-    packed_grads = jnp.pad(packed_grads, ((0, 0), (0, held - flat))).reshape(-1, LANES)
-    one_parts, qkv_swapped, out_swapped, small_swapped = exchange(
+    packed_grads = side_by_side([g.reshape(n_dp, -1) for g in small_grads], sizes, held)
+    packed_grads = packed_grads.reshape(-1, LANES)
+    one_part, down_parts = lax.optimization_barrier((one_part.astype(bf16), down_parts))
+    down_sum = down_blocks[0].astype(f32)
+    for part in down_parts:
+        down_sum = down_sum + part.astype(f32)
+    mixed = (first + down_sum + down_bias).astype(bf16)
+    one_parts, qkv_swapped, out_swapped, small_all = exchange(
         "sum_third",
         5,
         [
-            swap_tensor(one_part.astype(bf16).reshape(parts, padded, width)),
+            swap_tensor(one_part.reshape(parts, padded, width)),
             swap_dp(grad_qkv_w.astype(bf16), 1),
             swap_dp(grad_out_w.astype(bf16), 1),
-            swap_dp(packed_grads, 0),
         ],
-    )
-    (small_all,) = exchange("sum_small", 6, [gather_tensor(summed(small_swapped))])
+        packed_grads,
+    )
     hat_own, scale_own = normalized(inputs)
     grad_tokens = grad_first + norm_back(summed(one_parts), gain_one, hat_own, scale_own)
     small_sum = summed(small_all).reshape(held)
@@ -532,7 +610,7 @@
         done[6],
         summed(up_swapped),
         done[8],
-        down_w_sum,
+        summed(down_swapped),
         done[7],
     )
 

time: 375 us -> 337 us (0.90); the launches traced: 368 us -> 336 us
  Pallas kernels: 259 us -> 186 us
  waiting for transfers between devices: 0 us -> 27.6 us
  starting transfers between devices: 0 us -> 23.1 us
  local copies, waits for them, and re-layouts: 23.3 us -> 14.8 us
  other arithmetic: 24.8 us -> 33.2 us
  matrix products: 59.1 us -> 50.8 us
    pallas_call x7 -> x6, Pallas kernels: 259 us -> 186 us  [exchange(): pl.pallas_call(kernel, out_shape=tuple(shapes), in_specs=specs, out_specs...]
    ppermute x0 -> x6, waiting for transfers between devices: none -> 27.6 us  [permuted(): return lax.ppermute(block, 'tensor', [(j, (j + k) % n) for j in range(n)])]
    ppermute x0 -> x6, starting transfers between devices: none -> 23.1 us  [permuted(): return lax.ppermute(block, 'tensor', [(j, (j + k) % n) for j in range(n)])]
    unnamed x83 -> x78, local copies, waits for them, and re-layouts: 11.4 us -> 6.32 us
    convert_element_type x1, other arithmetic: 1.58 us -> 6.01 us  [body(): grad_scores = (probs_again * (grad_probs - inner)).astype(bf16)]
    reduce_sum x9 -> x7, other arithmetic: 11.9 us -> 9.01 us  [summed(): return jnp.sum(parts.astype(jnp.float32), axis=0)]
  transfers between devices with their start and end apart: 0 -> 6, of which waited for: 0 -> 4; matrix products, arithmetic and copies ran while one was open for 0% -> 8% of each run, Pallas kernels for 0% -> 0%
where the time goes in v2:
time: 337 us; the launch traced here: 336 us
  Pallas kernels  186 us (55%)
  matrix products  50.8 us (15%)
  other arithmetic  33.2 us (10%)
  waiting for transfers between devices  27.6 us (8%)
  starting transfers between devices  23.1 us (7%)
  local copies, waits for them, and re-layouts  14.8 us (4%)
    pallas_call x6, Pallas kernels, exchange(): pl.pallas_call(kernel, out_shape=tuple(shapes), in_specs=specs, out_specs...  186 us
    ppermute x6, waiting for transfers between devices, permuted(): return lax.ppermute(block, 'tensor', [(j, (j + k) % n) for j in range(n)])  27.6 us
    ppermute x6, starting transfers between devices, permuted(): return lax.ppermute(block, 'tensor', [(j, (j + k) % n) for j in range(n)])  23.1 us
    reduce_sum x7, other arithmetic, summed(): return jnp.sum(parts.astype(jnp.float32), axis=0)  9.01 us
    dot_general x1, matrix products, body(): jnp.einsum('pd,fd->pf', grad_rows, down_full, preferred_element_type=f32)  7.75 us
  transfers between devices with their start and end apart: 6, of which 4 were waited for; matrix products, arithmetic and copies ran while one was open for 8% of the time, Pallas kernels for 0%

profile of v2, /device:TPU:0, one launch (start us, length us, event | category | flops | bytes accessed | tf_op | source)
XLA Modules:
  0.0 336.3 jit_solution(6727853669668012906)
XLA Ops:
  2.5 1.8 pad.79.refs_0_
  4.4 1.4 add_bitcast_fusion.refs_3_
  5.7 30.9 %gather_first.1 = (bf16[4,160,1024]{2,1,0:T(8,128)(2,1)}, bf16[3,1024,256]{2,1,0:T(8,128)(2,1)}, bf16[256,1024]{1,0:T(8,128)(2,1)}, bf16[128,128]{1,0:T(8,128)(2,1)}) custom-call(bf16[160,1024]{1,0:T(8,128)(2,1)} %pad.79.refs_0_, bf16[3,128,256]{2,1,0:T(8,128)(2,1)} %refs_1_.2, bf16[256,128]{1,0:T(8,128)(2,1)} %refs_2_.2, ...), custom_call_target="tpu_custom_call" | custom-call | bytes 6881280 | tf_op jit(solution)/shard_map/gather_first/pallas_call | solution.py:296
  36.7 1.4 collective-permute-start.2
  38.0 12.2 %collective-permute-start.1 = (bf16[160,1024]{1,0:T(8,128)(2,1)S(1)}, bf16[160,1024]{1,0:T(8,128)(2,1)S(1)}, u32[]{:S(2)}, u32[]{:S(2)}) collective-permute-start(bf16[160,1024]{1,0:T(8,128)(2,1)S(1)} %pad.89), channel_id=1, source_target_pairs={{0,2},{1,3},{2,0},{3,1},{4,6},{5,7},{6,4},{7,5},{8,10},{9,11},{10,... | collective-permute-start | bytes 983048 | tf_op jit(solution)/shard_map/ppermute | solution.py:62
  50.3 1.9 collective-permute-start
  52.3 1.6 convert_reduce_fusion.8
  54.0 1.8 multiply_reduce_fusion.1
  57.4 1.4 convolution_bitcast_fusion
  59.5 1.6 fusion.45
  62.0 1.8 copy-done
  63.8 1.3 fusion.22
  66.0 1.6 convolution_convert_fusion.3
  67.7 10.6 %collective-permute-done.1 = bf16[160,1024]{1,0:T(8,128)(2,1)S(1)} collective-permute-done((bf16[160,1024]{1,0:T(8,128)(2,1)S(1)}, bf16[160,1024]{1,0:T(8,128)(2,1)S(1)}, u32[]{:S(2)}, u32[]{:S(2)}) %collective-permute-start.1) | collective-permute-done | bytes 327712 | tf_op jit(solution)/shard_map/ppermute | solution.py:62
  78.2 30.5 %sum_branch.1 = (bf16[4,160,1024]{2,1,0:T(8,128)(2,1)}, bf16[1024,1024]{1,0:T(8,128)(2,1)}, bf16[1024,1024]{1,0:T(8,128)(2,1)}) custom-call(bf16[4,160,1024]{2,1,0:T(8,128)(2,1)} %bitcast.139, bf16[128,1024]{1,0:T(8,128)(2,1)} %refs_1_.3, bf16[1024,128]{1,0:T(8,128)(2,1)} %refs_2_.3), custom_call_target="tpu_custom_call" | custom-call | bytes 11010048 | tf_op jit(solution)/shard_map/sum_branch/pallas_call | solution.py:296
  108.7 1.6 convert_reduce_fusion.7
  111.8 25.5 %gather_second.1 = bf16[4,160,1024]{2,1,0:T(8,128)(2,1)} custom-call(bf16[160,1024]{1,0:T(8,128)(2,1)} %add_convert_fusion.2.refs_0_), custom_call_target="tpu_custom_call" | custom-call | bytes 2621440 | tf_op jit(solution)/shard_map/gather_second/pallas_call | solution.py:296
  137.4 3.7 %fusion.46 = f32[640,1024]{1,0:T(8,128)S(1)} fusion(bf16[640,1024]{1,0:T(8,128)(2,1)} %bitcast.155, bf16[1024,1024]{1,0:T(8,128)(2,1)} %get-tuple-element.53), kind=kOutput, calls=%fused_computation.153 | convolution fusion | flops 1342177280 | bytes 6029312 | tf_op jit(solution)/shard_map/dot_general | solution.py:480
  141.1 7.8 %convert_reduce_fusion.6 = (f32[1024]{0:T(1024)S(1)}, bf16[640,1024]{1,0:T(8,128)(2,1)S(1)}, f32[640,1024]{1,0:T(8,128)S(1)}) fusion(f32[640,1024]{1,0:T(8,128)S(1)} %fusion.46, f32[1024]{0:T(1024)S(1)} %dynamic_slice.11, bf16[640,1024]{1,0:T(8,128)(2,1)S(1)} %constant_dynamic-update-slice_fusion, bf16[1024,1024]{1,0:T(8,128)(2,1)S(1)} %copy-done.32), kind=kOutput, calls=%fused_computation.25 | convolution fusion | flops 1391328256 | bytes 9969664 | tf_op jit(solution)/shard_map/pd,fd->pf/dot_general | solution.py:484
  149.5 2.6 convolution_convert_fusion.4
  152.1 3.2 convolution_convert_fusion.refs_1_
  155.3 2.6 convolution_convert_fusion.5
  158.0 3.2 convolution_convert_fusion.1.refs_1_
  161.2 32.1 %sum_second.1 = (bf16[4,160,1024]{2,1,0:T(8,128)(2,1)}, bf16[8,128,1024]{2,1,0:T(8,128)(2,1)}) custom-call(bf16[4,160,1024]{2,1,0:T(8,128)(2,1)} %bitcast.157, bf16[1024,1024]{1,0:T(8,128)(2,1)} %convolution_convert_fusion.1.refs_1_), custom_call_target="tpu_custom_call" | custom-call | bytes 6815744 | tf_op jit(solution)/shard_map/sum_second/pallas_call | solution.py:296
  193.3 1.9 convert_reduce_fusion.2
  195.6 1.3 convert_reduce_fusion.12
  196.9 31.5 %gather_third.1 = (bf16[4,160,1024]{2,1,0:T(8,128)(2,1)}, bf16[8,1024,128]{2,1,0:T(8,128)(2,1)}) custom-call(bf16[160,1024]{1,0:T(8,128)(2,1)} %get-tuple-element.101.refs_0_, bf16[1024,1024]{1,0:T(8,128)(2,1)} %convolution_convert_fusion.refs_1_), custom_call_target="tpu_custom_call" | custom-call | bytes 6815744 | tf_op jit(solution)/shard_map/gather_third/pallas_call | solution.py:296
  228.4 2.2 convolution_convert_fusion.7
  230.6 4.8 %convert_reduce_fusion.13 = (f32[4,64]{1,0:T(4,128)S(1)}, bf16[4,64,640]{2,1,0:T(8,128)(2,1)}) fusion(bf16[640,4,64]{0,2,1:T(8,128)(2,1)S(1)} %bitcast.148, f32[4,640,640]{1,2,0:T(8,128)} %copy-done, f32[4,640]{1,0:T(4,128)S(1)} %log_add_fusion), kind=kOutput, calls=%fused_computation.77 | convolution fusion | flops 213483264 | bytes 7220224 | tf_op jit(solution)/shard_map/hqk,qhe->khe/dot_general | solution.py:525
  235.5 4.0 %multiply_reduce_fusion = (f32[4,640]{1,0:T(4,128)S(1)}, f32[4,640,640]{1,2,0:T(8,128)}) fusion(f32[4,640,640]{1,2,0:T(8,128)S(1)} %bitcast.136, f32[4,640]{1,0:T(4,128)S(1)} %log_add_fusion, bf16[640,4,64]{0,2,1:T(8,128)(2,1)S(1)} %bitcast.149, f32[640,4,64]{0,2,1:T(8,128)S(1)} %bitcast.147, f32[4,64]{1,0:T(4,128)S(1)} %add.270), kind=kOutput, calls=%fused_computation.1 | convolution fusion | flops 214955520 | bytes 14111744 | tf_op jit(solution)/shard_map/qhe,khe->hqk/dot_general | solution.py:521
  239.5 1.1 convert_reduce_fusion.1
  241.4 1.8 collective-permute-start.4
  243.2 5.6 %collective-permute-start.3 = (bf16[160,1024]{1,0:T(8,128)(2,1)S(1)}, bf16[160,1024]{1,0:T(8,128)(2,1)}, u32[]{:S(2)}, u32[]{:S(2)}) collective-permute-start(bf16[160,1024]{1,0:T(8,128)(2,1)S(1)} %get-tuple-element.113), channel_id=1, source_target_pairs={{0,1},{1,2},{2,3},{3,0},{4,5},{5,6},{6,7},{7,4},{8,9},{9,10},{10,1... | collective-permute-start | bytes 983048 | tf_op jit(solution)/shard_map/ppermute | solution.py:62
  248.9 1.1 convert_reduce_fusion
  251.3 1.4 convolution_convert_fusion.6.refs_2_
  252.7 4.4 %collective-permute-done.4 = bf16[160,1024]{1,0:T(8,128)(2,1)} collective-permute-done((bf16[160,1024]{1,0:T(8,128)(2,1)}, bf16[160,1024]{1,0:T(8,128)(2,1)}, u32[]{:S(2)}, u32[]{:S(2)}) %collective-permute-start.4) | collective-permute-done | bytes 327712 | tf_op jit(solution)/shard_map/ppermute | solution.py:62
  257.1 8.3 %collective-permute-done.3 = bf16[160,1024]{1,0:T(8,128)(2,1)} collective-permute-done((bf16[160,1024]{1,0:T(8,128)(2,1)S(1)}, bf16[160,1024]{1,0:T(8,128)(2,1)}, u32[]{:S(2)}, u32[]{:S(2)}) %collective-permute-start.3) | collective-permute-done | bytes 327712 | tf_op jit(solution)/shard_map/ppermute | solution.py:62
  265.4 6.0 %multiply_convert_fusion = bf16[4,640,640]{1,2,0:T(8,128)(2,1)S(1)} fusion(f32[4,640,640]{1,2,0:T(8,128)} %get-tuple-element.136, f32[4,640,640]{1,2,0:T(8,128)} %copy-done, f32[4,640]{1,0:T(4,128)S(1)} %get-tuple-element.135, f32[4,640]{1,0:T(4,128)S(1)} %log_add_fusion), kind=kLoop, calls=%fused_computation | loop fusion | flops 6553600 | bytes 16404480 | tf_op jit(solution)/shard_map/convert_element_type | solution.py:532
  271.4 1.2 fusion.18
  275.9 3.7 %bitcast_convert_fusion = (bf16[640,1024]{1,0:T(8,128)(2,1)}, f32[640,1024,1]{1,0,2:T(8,128)S(1)}) fusion(bf16[3,1024,256]{2,1,0:T(8,128)(2,1)} %get-tuple-element.45, bf16[1,640,256]{2,1,0:T(8,128)(2,1)S(1)} %copy-done.26, bf16[1,640,256]{2,1,0:T(8,128)(2,1)S(1)} %copy.34, bf16[1,640,256]{2,1,0:T(8,128)(2,1)S(1)} %copy.33), kind=kOutput, calls=%fused_computation.20 | convolution fusion | flops 1008271360 | bytes 6488064 | tf_op jit(solution)/shard_map/cpe,cde->pd/dot_general | solution.py:562
  281.1 3.7 %fusion.14.refs_1_ = bf16[3,1024,256]{2,1,0:T(8,128)(2,1)} fusion(bf16[640,1024]{1,0:T(8,128)(2,1)S(1)} %copy-done.17, bf16[1,640,256]{2,1,0:T(8,128)(2,1)S(1)} %copy-done.26, bf16[1,640,256]{2,1,0:T(8,128)(2,1)} %copy-done.28, bf16[1,640,256]{2,1,0:T(8,128)(2,1)} %copy-done.27), kind=kOutput, calls=%fused_computation.52 | convolution fusion | flops 1008402432 | bytes 3866624 | tf_op jit(solution)/shard_map/pd,cpe->cde/dot_general | solution.py:552
  284.8 4.3 %collective-permute-done.5 = bf16[160,1024]{1,0:T(8,128)(2,1)} collective-permute-done((bf16[160,1024]{1,0:T(8,128)(2,1)}, bf16[160,1024]{1,0:T(8,128)(2,1)}, u32[]{:S(2)}, u32[]{:S(2)}) %collective-permute-start.5) | collective-permute-done | bytes 327712 | tf_op jit(solution)/shard_map/ppermute | solution.py:62
  289.1 35.2 %sum_third.1 = (bf16[4,160,1024]{2,1,0:T(8,128)(2,1)}, bf16[8,3,128,256]{3,2,1,0:T(8,128)(2,1)}, bf16[8,256,128]{2,1,0:T(8,128)(2,1)}, f32[4,16,128]{2,1,0:T(8,128)}) custom-call(bf16[4,160,1024]{2,1,0:T(8,128)(2,1)} %bitcast.154, bf16[3,1024,256]{2,1,0:T(8,128)(2,1)} %fusion.14.refs_1_, bf16[256,1024]{1,0:T(8,128)(2,1)} %convolution_convert_fusion.6.refs_2_, ...), custom_call_target="tpu_custom_call" | custom-call | bytes 6815744 | tf_op jit(solution)/shard_map/sum_third/pallas_call | solution.py:296
  326.8 1.6 convert_reduce_fusion.5
  328.5 1.8 convert_reduce_fusion.9
  330.2 1.1 convert_element_type.286
  332.8 1.4 copy.38
  334.2 2.0 fusion.34
  (142 shorter events, 19.3 us)
Async XLA Ops:
  0.6 51.6 %copy-start.5 = (bf16[145,1,1024]{2,0,1:T(8,128)(2,1)S(1)}, bf16[145,1,1024]{2,0,1:T(8,128)(2,1)}, u32[]{:S(2)}) copy-start(bf16[145,1,1024]{2,0,1:T(8,128)(2,1)} %param.14) | copy-start | bytes 890884
  2.5 62.6 %copy-start.8 = (bf16[160,1024]{1,0:T(8,128)(2,1)}, bf16[160,1024]{1,0:T(8,128)(2,1)S(1)}, u32[]{:S(2)}) copy-start(bf16[160,1024]{1,0:T(8,128)(2,1)S(1)} %pad.89) | copy-start | bytes 983044
  36.6 19.2 %copy-start.30 = (bf16[128,128]{1,0:T(8,128)(2,1)S(1)}, bf16[128,128]{1,0:T(8,128)(2,1)}, u32[]{:S(2)}) copy-start(bf16[128,128]{1,0:T(8,128)(2,1)} %get-tuple-element.48) | copy-start | bytes 98308
  36.7 19.3 %copy-start.1 = (bf16[4,160,1024]{2,1,0:T(8,128)(2,1)S(1)}, bf16[4,160,1024]{2,1,0:T(8,128)(2,1)}, u32[]{:S(2)}) copy-start(bf16[4,160,1024]{2,1,0:T(8,128)(2,1)} %get-tuple-element.47) | copy-start | bytes 3932164
  36.7 31.0 %collective-permute-start.2 = (bf16[160,1024]{1,0:T(8,128)(2,1)S(1)}, bf16[160,1024]{1,0:T(8,128)(2,1)S(1)}, u32[]{:S(2)}, u32[]{:S(2)}) collective-permute-start(bf16[160,1024]{1,0:T(8,128)(2,1)S(1)} %pad.89), channel_id=1, source_target_pairs={{0,3},{1,0},{2,1},{3,2},{4,7},{5,4},{6,5},{7,6},{8,11},{9,8},{10,9... | collective-permute-start | bytes 983048 | tf_op jit(solution)/shard_map/ppermute | solution.py:62
  38.0 40.2 %collective-permute-start.1 = (bf16[160,1024]{1,0:T(8,128)(2,1)S(1)}, bf16[160,1024]{1,0:T(8,128)(2,1)S(1)}, u32[]{:S(2)}, u32[]{:S(2)}) collective-permute-start(bf16[160,1024]{1,0:T(8,128)(2,1)S(1)} %pad.89), channel_id=1, source_target_pairs={{0,2},{1,3},{2,0},{3,1},{4,6},{5,7},{6,4},{7,5},{8,10},{9,11},{10,... | collective-permute-start | bytes 983048 | tf_op jit(solution)/shard_map/ppermute | solution.py:62
  50.3 28.0 %collective-permute-start = (bf16[160,1024]{1,0:T(8,128)(2,1)S(1)}, bf16[160,1024]{1,0:T(8,128)(2,1)S(1)}, u32[]{:S(2)}, u32[]{:S(2)}) collective-permute-start(bf16[160,1024]{1,0:T(8,128)(2,1)S(1)} %pad.89), channel_id=1, source_target_pairs={{0,1},{1,2},{2,3},{3,0},{4,5},{5,6},{6,7},{7,4},{8,9},{9,10},{10,1... | collective-permute-start | bytes 983048 | tf_op jit(solution)/shard_map/ppermute | solution.py:62
  56.0 1.4 copy-start.33
  56.5 2.3 copy-start.16
  58.9 2.2 copy-start.6
  59.0 2.1 copy-start.3
  59.0 3.0 copy-start.10
  61.1 2.7 copy-start
  63.8 2.2 copy-start.25
  65.2 45.2 %copy-start.23 = (bf16[4,64,640]{2,1,0:T(8,128)(2,1)}, bf16[4,64,640]{2,1,0:T(8,128)(2,1)S(1)}, u32[]{:S(2)}) copy-start(bf16[4,64,640]{2,1,0:T(8,128)(2,1)S(1)} %fusion.22) | copy-start | bytes 983044
  110.4 26.9 %copy-start.29 = (bf16[640,1024]{1,0:T(8,128)(2,1)S(1)}, bf16[640,1024]{1,0:T(8,128)(2,1)}, u32[]{:S(2)}) copy-start(bf16[640,1024]{1,0:T(8,128)(2,1)} %constant_dynamic-update-slice_fusion.3) | copy-start | bytes 3932164
  137.4 3.7 %copy-start.32 = (bf16[1024,1024]{1,0:T(8,128)(2,1)S(1)}, bf16[1024,1024]{1,0:T(8,128)(2,1)}, u32[]{:S(2)}) copy-start(bf16[1024,1024]{1,0:T(8,128)(2,1)} %get-tuple-element.57) | copy-start | bytes 6291460
  152.1 3.2 copy-start.31
  155.3 2.6 copy-start.21
  193.3 2.3 copy-start.9
  195.6 39.8 %slice-start = ((s8[6553600]{0:T(1024)(128)(4,1)}), s8[2359296]{0:T(1024)(128)(4,1)S(1)}, s32[]{:S(2)}) async-start(s8[6553600]{0:T(1024)(128)(4,1)} %bitcast.135), calls=%async_computation | async-start | bytes 4718592
  228.4 7.1 %slice-start.1 = ((s8[6553600]{0:T(1024)(128)(4,1)}), s8[4194304]{0:T(1024)(128)(4,1)S(1)}, s32[]{:S(2)}) async-start(s8[6553600]{0:T(1024)(128)(4,1)} %bitcast.135), calls=%async_computation.1 | async-start | bytes 8388608
  230.6 4.9 %copy-start.11 = (f32[1,640,256]{1,2,0:T(8,128)S(1)}, f32[1,640,256]{1,2,0:T(8,128)}, u32[]{:S(2)}) copy-start(f32[1,640,256]{1,2,0:T(8,128)} %copy-done.10) | copy-start | bytes 1966084
  235.5 4.0 %copy-start.13 = (bf16[8,128,1024]{2,1,0:T(8,128)(2,1)S(1)}, bf16[8,128,1024]{2,1,0:T(8,128)(2,1)}, u32[]{:S(2)}) copy-start(bf16[8,128,1024]{2,1,0:T(8,128)(2,1)} %get-tuple-element.74) | copy-start | bytes 6291460
  235.5 5.2 %copy-start.18 = (bf16[640,1024]{1,0:T(8,128)(2,1)S(1)}, bf16[640,1024]{1,0:T(8,128)(2,1)}, u32[]{:S(2)}) copy-start(bf16[640,1024]{1,0:T(8,128)(2,1)} %convolution_convert_fusion.4) | copy-start | bytes 3932164
  239.5 9.4 %copy-start.14 = (bf16[8,1024,128]{2,1,0:T(8,128)(2,1)S(1)}, bf16[8,1024,128]{2,1,0:T(8,128)(2,1)}, u32[]{:S(2)}) copy-start(bf16[8,1024,128]{2,1,0:T(8,128)(2,1)} %get-tuple-element.75) | copy-start | bytes 6291460
  240.6 9.6 %copy-start.22 = (bf16[4,64,640]{2,1,0:T(8,128)(2,1)S(1)}, bf16[4,64,640]{2,1,0:T(8,128)(2,1)}, u32[]{:S(2)}) copy-start(bf16[4,64,640]{2,1,0:T(8,128)(2,1)} %get-tuple-element.140) | copy-start | bytes 983044
  240.6 10.7 %copy-start.20 = (bf16[4,160,1024]{2,1,0:T(8,128)(2,1)S(1)}, bf16[4,160,1024]{2,1,0:T(8,128)(2,1)}, u32[]{:S(2)}) copy-start(bf16[4,160,1024]{2,1,0:T(8,128)(2,1)} %get-tuple-element.60) | copy-start | bytes 3932164
  240.6 10.7 %copy-start.24 = (bf16[4,64,640]{2,1,0:T(8,128)(2,1)S(1)}, bf16[4,64,640]{2,1,0:T(8,128)(2,1)}, u32[]{:S(2)}) copy-start(bf16[4,64,640]{2,1,0:T(8,128)(2,1)} %copy-done.23) | copy-start | bytes 983044
  241.4 15.7 %collective-permute-start.4 = (bf16[160,1024]{1,0:T(8,128)(2,1)}, bf16[160,1024]{1,0:T(8,128)(2,1)}, u32[]{:S(2)}, u32[]{:S(2)}) collective-permute-start(bf16[160,1024]{1,0:T(8,128)(2,1)} %get-tuple-element.112), channel_id=1, source_target_pairs={{0,3},{1,0},{2,1},{3,2},{4,7},{5,4},{6,5},{7,6},{8,11},{9,8},{10,9... | collective-permute-start | bytes 983048 | tf_op jit(solution)/shard_map/ppermute | solution.py:62
  243.2 22.1 %collective-permute-start.3 = (bf16[160,1024]{1,0:T(8,128)(2,1)S(1)}, bf16[160,1024]{1,0:T(8,128)(2,1)}, u32[]{:S(2)}, u32[]{:S(2)}) collective-permute-start(bf16[160,1024]{1,0:T(8,128)(2,1)S(1)} %get-tuple-element.113), channel_id=1, source_target_pairs={{0,1},{1,2},{2,3},{3,0},{4,5},{5,6},{6,7},{7,4},{8,9},{9,10},{10,1... | collective-permute-start | bytes 983048 | tf_op jit(solution)/shard_map/ppermute | solution.py:62
  265.4 6.0 %copy-start.4 = (f32[1,640,256]{1,2,0:T(8,128)S(1)}, f32[1,640,256]{1,2,0:T(8,128)}, u32[]{:S(2)}) copy-start(f32[1,640,256]{1,2,0:T(8,128)} %copy-done.3) | copy-start | bytes 1966084
  271.4 1.2 copy-start.7
  272.6 1.3 copy-start.19
  272.6 3.3 copy-start.26
  275.0 0.7 copy-start.27
  275.2 0.8 copy-start.28
  275.2 4.5 %copy-start.2 = (bf16[4,160,1024]{2,1,0:T(8,128)(2,1)S(1)}, bf16[4,160,1024]{2,1,0:T(8,128)(2,1)}, u32[]{:S(2)}) copy-start(bf16[4,160,1024]{2,1,0:T(8,128)(2,1)} %get-tuple-element.47) | copy-start | bytes 3932164
  275.2 13.9 %collective-permute-start.5 = (bf16[160,1024]{1,0:T(8,128)(2,1)}, bf16[160,1024]{1,0:T(8,128)(2,1)}, u32[]{:S(2)}, u32[]{:S(2)}) collective-permute-start(bf16[160,1024]{1,0:T(8,128)(2,1)} %get-tuple-element.111), channel_id=1, source_target_pairs={{0,2},{1,3},{2,0},{3,1},{4,6},{5,7},{6,4},{7,5},{8,10},{9,11},{10,... | collective-permute-start | bytes 983048 | tf_op jit(solution)/shard_map/ppermute | solution.py:62
  279.6 1.5 copy-start.17
  325.1 6.2 %copy-start.15 = (bf16[8,3,128,256]{3,2,1,0:T(8,128)(2,1)S(1)}, bf16[8,3,128,256]{3,2,1,0:T(8,128)(2,1)}, u32[]{:S(2)}) copy-start(bf16[8,3,128,256]{3,2,1,0:T(8,128)(2,1)} %get-tuple-element.72) | copy-start | bytes 4718596
  330.2 2.4 copy-start.12

commit v3 on v2

--- a/solution.py
+++ b/solution.py
@@ -107,7 +107,7 @@
         srcs = refs[:count]
         dsts = refs[count + extra : 2 * count + extra]
         scratch = refs[2 * (count + extra) :]
-        own_sem, send, recv, fsend, frecv, ssend, srecv, tsend, trecv = scratch[:9]
+        own_sem, send, recv, fsend, frecv, ssend, srecv, tsend, trecv, rsend = scratch[:10]
         t = lax.axis_index("tensor")
         d = lax.axis_index("dp")
         core = lax.rem(d, 2)
@@ -195,7 +195,7 @@
 
         if extra:
             small_in, small_out = refs[count], refs[2 * count + 1]
-            small_got, small_sum, dsend, drecv, esend, erecv = scratch[9:]
+            small_got, small_sum, dsend, drecv, esend, erecv = scratch[10:]
             view = at_dim(0, small_rows)
 
             def small_swap(k, owner):
@@ -215,9 +215,24 @@
         def of(kind):
             return [i for i in range(count) if items[i].kind == kind]
 
+        def relayed(i):
+            return n_t == 4 and items[i].src is whole
+
+        def relay_copy(i):
+            block = items[i].dst(dsts[i], 2 if items[i].turned else (2 - t) * 3)
+            landing = items[i].dst(dsts[i], 2 * t - 1 if items[i].turned else (2 - t) * 3)
+            k = 2 * t - 1
+            return remote(block, landing, rsend.at[i], trecv.at[i, k], d, (t - 1) * 3)
+
+        def unless_relayed(i, k, act):
+            if relayed(i) and k != 2:
+                pl.when(t != (0 if k == 3 else 3))(act)
+            else:
+                act()
+
         for k in (2, 3, 1) if n_t == 4 else range(1, n_t):
             for i in of("tensor"):
-                tensor_copy(i, k, t).start()
+                unless_relayed(i, k, lambda i=i, k=k: tensor_copy(i, k, t).start())
         for i in of("gather"):
             loop(1, chips, lambda k, i=i: gather_copy(i, k, d).start())
             forward_copy(i, 0, d, True).start()
@@ -233,6 +248,20 @@
                 small_gather(k, t).start()
             small_out[t] = small_sum[...]
 
+        middle = (t == 1) | (t == 2)
+
+        def relay_all():
+            for i in of("tensor"):
+                if relayed(i):
+                    tensor_copy(i, 2, lax.rem(t + n_t - 2, n_t)).wait_recv()
+
+                    @pl.when(middle)
+                    def _(i=i):
+                        relay_copy(i).start()
+
+        if not with_gather:
+            relay_all()
+
         def came(k):
             return lax.rem(chip + chips - k, chips) * 2
 
@@ -243,6 +272,8 @@
                 forward_copy(i, k, came(k) + core, False).start()
 
             loop(1, chips, pass_on)
+        if with_gather:
+            relay_all()
         for i in of("gather"):
             other = 1 - core
             forward_copy(i, 0, came(0) + other, True).wait_recv()
@@ -263,8 +294,15 @@
             loop(1, n_dp, end)
         for i in of("tensor"):
             for k in range(1, n_t):
-                tensor_copy(i, k, lax.rem(t + n_t - k, n_t)).wait_recv()
-                tensor_copy(i, k, t).wait_send()
+                if not (relayed(i) and k == 2):
+                    tensor_copy(i, k, lax.rem(t + n_t - k, n_t)).wait_recv()
+                unless_relayed(i, k, lambda i=i, k=k: tensor_copy(i, k, t).wait_send())
+            if relayed(i):
+
+                @pl.when(middle)
+                def _(i=i):
+                    relay_copy(i).wait_send()
+
         for i in range(count):
             own_copy(i).wait()
         if extra:
@@ -308,6 +346,7 @@
             dma((count, n_dp)),
             dma((count, n_t)),
             dma((count, n_t)),
+            dma((count,)),
             *own_scratch,
         ],
         compiler_params=pltpu.CompilerParams(collective_id=number, has_side_effects=True),

time: 337 us -> 318 us (0.944)
  starting transfers between devices: 23.1 us -> 5.84 us
  Pallas kernels: 186 us -> 181 us
  waiting for transfers between devices: 27.6 us -> 31.2 us
    ppermute x6, starting transfers between devices: 23.1 us -> 5.84 us  [permuted(): return lax.ppermute(block, 'tensor', [(j, (j + k) % n) for j in range(n)])]
    pallas_call x6, Pallas kernels: 186 us -> 181 us  [exchange(): pl.pallas_call(kernel, out_shape=tuple(shapes), in_specs=specs, out_specs...]
    ppermute x6, waiting for transfers between devices: 27.6 us -> 31.2 us  [permuted(): return lax.ppermute(block, 'tensor', [(j, (j + k) % n) for j in range(n)])]
where the time goes in v3:
time: 318 us
  Pallas kernels  181 us (57%)
  matrix products  50.8 us (16%)
  other arithmetic  33.2 us (10%)
  waiting for transfers between devices  31.2 us (10%)
  local copies, waits for them, and re-layouts  14.1 us (4%)
  starting transfers between devices  5.84 us (2%)
    pallas_call x6, Pallas kernels, exchange(): pl.pallas_call(kernel, out_shape=tuple(shapes), in_specs=specs, out_specs...  181 us
    ppermute x6, waiting for transfers between devices, permuted(): return lax.ppermute(block, 'tensor', [(j, (j + k) % n) for j in range(n)])  31.2 us
    reduce_sum x7, other arithmetic, summed(): return jnp.sum(parts.astype(jnp.float32), axis=0)  9.01 us
    dot_general x1, matrix products, body(): jnp.einsum('pd,fd->pf', grad_rows, down_full, preferred_element_type=f32)  7.75 us
  transfers between devices with their start and end apart: 6, of which 4 were waited for; matrix products, arithmetic and copies ran while one was open for 8% of the time, Pallas kernels for 0%

profile of v3, /device:TPU:0, one launch (start us, length us, event | category | flops | bytes accessed | tf_op | source)
XLA Modules:
  0.0 317.8 jit_solution(16903851112009327605)
XLA Ops:
  1.4 1.1 bitcast_select_fusion
  2.5 1.8 pad.79.refs_0_
  4.4 1.4 add_bitcast_fusion.refs_3_
  5.7 29.9 %gather_first.1 = (bf16[4,160,1024]{2,1,0:T(8,128)(2,1)}, bf16[3,1024,256]{2,1,0:T(8,128)(2,1)}, bf16[256,1024]{1,0:T(8,128)(2,1)}, bf16[128,128]{1,0:T(8,128)(2,1)}) custom-call(bf16[160,1024]{1,0:T(8,128)(2,1)} %pad.79.refs_0_, bf16[3,128,256]{2,1,0:T(8,128)(2,1)} %refs_1_.2, bf16[256,128]{1,0:T(8,128)(2,1)} %refs_2_.2, ...), custom_call_target="tpu_custom_call" | custom-call | bytes 6881280 | tf_op jit(solution)/shard_map/gather_first/pallas_call | solution.py:334
  35.6 1.5 collective-permute-start.2
  38.3 1.6 convert_reduce_fusion.8
  40.0 1.8 multiply_reduce_fusion.1
  43.4 1.4 convolution_bitcast_fusion
  45.5 1.6 fusion.45
  48.0 1.8 copy-done
  49.8 1.3 fusion.22
  52.0 1.6 convolution_convert_fusion.3
  53.6 11.7 %collective-permute-done.1 = bf16[160,1024]{1,0:T(8,128)(2,1)S(1)} collective-permute-done((bf16[160,1024]{1,0:T(8,128)(2,1)S(1)}, bf16[160,1024]{1,0:T(8,128)(2,1)S(1)}, u32[]{:S(2)}, u32[]{:S(2)}) %collective-permute-start.1) | collective-permute-done | bytes 327712 | tf_op jit(solution)/shard_map/ppermute | solution.py:62
  65.3 30.1 %sum_branch.1 = (bf16[4,160,1024]{2,1,0:T(8,128)(2,1)}, bf16[1024,1024]{1,0:T(8,128)(2,1)}, bf16[1024,1024]{1,0:T(8,128)(2,1)}) custom-call(bf16[4,160,1024]{2,1,0:T(8,128)(2,1)} %bitcast.139, bf16[128,1024]{1,0:T(8,128)(2,1)} %refs_1_.3, bf16[1024,128]{1,0:T(8,128)(2,1)} %refs_2_.3), custom_call_target="tpu_custom_call" | custom-call | bytes 11010048 | tf_op jit(solution)/shard_map/sum_branch/pallas_call | solution.py:334
  95.5 1.6 convert_reduce_fusion.7
  98.6 26.8 %gather_second.1 = bf16[4,160,1024]{2,1,0:T(8,128)(2,1)} custom-call(bf16[160,1024]{1,0:T(8,128)(2,1)} %add_convert_fusion.2.refs_0_), custom_call_target="tpu_custom_call" | custom-call | bytes 2621440 | tf_op jit(solution)/shard_map/gather_second/pallas_call | solution.py:334
  125.6 3.7 %fusion.46 = f32[640,1024]{1,0:T(8,128)S(1)} fusion(bf16[640,1024]{1,0:T(8,128)(2,1)} %bitcast.155, bf16[1024,1024]{1,0:T(8,128)(2,1)} %get-tuple-element.53), kind=kOutput, calls=%fused_computation.153 | convolution fusion | flops 1342177280 | bytes 6029312 | tf_op jit(solution)/shard_map/dot_general | solution.py:519
  129.2 7.8 %convert_reduce_fusion.6 = (f32[1024]{0:T(1024)S(1)}, bf16[640,1024]{1,0:T(8,128)(2,1)S(1)}, f32[640,1024]{1,0:T(8,128)S(1)}) fusion(f32[640,1024]{1,0:T(8,128)S(1)} %fusion.46, f32[1024]{0:T(1024)S(1)} %dynamic_slice.11, bf16[640,1024]{1,0:T(8,128)(2,1)S(1)} %constant_dynamic-update-slice_fusion, bf16[1024,1024]{1,0:T(8,128)(2,1)S(1)} %copy-done.32), kind=kOutput, calls=%fused_computation.25 | convolution fusion | flops 1391328256 | bytes 9969664 | tf_op jit(solution)/shard_map/pd,fd->pf/dot_general | solution.py:523
  137.7 2.6 convolution_convert_fusion.4
  140.3 3.2 %convolution_convert_fusion.refs_1_ = bf16[1024,1024]{1,0:T(8,128)(2,1)} fusion(bf16[640,1024]{1,0:T(8,128)(2,1)S(1)} %multiply_convert_fusion.1, bf16[640,1024]{1,0:T(8,128)(2,1)S(1)} %constant_dynamic-update-slice_fusion), kind=kOutput, calls=%fused_computation.45 | convolution fusion | flops 1343225856 | bytes 4718592 | tf_op jit(solution)/shard_map/pf,pd->fd/dot_general | solution.py:522
  143.5 2.6 convolution_convert_fusion.5
  146.1 3.2 %convolution_convert_fusion.1.refs_1_ = bf16[1024,1024]{1,0:T(8,128)(2,1)} fusion(bf16[640,1024]{1,0:T(8,128)(2,1)S(1)} %bitcast.156, bf16[640,1024]{1,0:T(8,128)(2,1)S(1)} %get-tuple-element.104), kind=kOutput, calls=%fused_computation.46 | convolution fusion | flops 1343225856 | bytes 4718592 | tf_op jit(solution)/shard_map/pd,pf->df/dot_general | solution.py:526
  149.4 27.2 %sum_second.1 = (bf16[4,160,1024]{2,1,0:T(8,128)(2,1)}, bf16[8,128,1024]{2,1,0:T(8,128)(2,1)}) custom-call(bf16[4,160,1024]{2,1,0:T(8,128)(2,1)} %bitcast.157, bf16[1024,1024]{1,0:T(8,128)(2,1)} %convolution_convert_fusion.1.refs_1_), custom_call_target="tpu_custom_call" | custom-call | bytes 6815744 | tf_op jit(solution)/shard_map/sum_second/pallas_call | solution.py:334
  176.6 1.9 convert_reduce_fusion.2
  179.0 1.3 convert_reduce_fusion.12
  180.3 31.9 %gather_third.1 = (bf16[4,160,1024]{2,1,0:T(8,128)(2,1)}, bf16[8,1024,128]{2,1,0:T(8,128)(2,1)}) custom-call(bf16[160,1024]{1,0:T(8,128)(2,1)} %get-tuple-element.101.refs_0_, bf16[1024,1024]{1,0:T(8,128)(2,1)} %convolution_convert_fusion.refs_1_), custom_call_target="tpu_custom_call" | custom-call | bytes 6815744 | tf_op jit(solution)/shard_map/gather_third/pallas_call | solution.py:334
  212.2 2.2 convolution_convert_fusion.7
  214.4 4.8 %convert_reduce_fusion.13 = (f32[4,64]{1,0:T(4,128)S(1)}, bf16[4,64,640]{2,1,0:T(8,128)(2,1)}) fusion(bf16[640,4,64]{0,2,1:T(8,128)(2,1)S(1)} %bitcast.148, f32[4,640,640]{1,2,0:T(8,128)} %copy-done, f32[4,640]{1,0:T(4,128)S(1)} %log_add_fusion), kind=kOutput, calls=%fused_computation.77 | convolution fusion | flops 213483264 | bytes 7220224 | tf_op jit(solution)/shard_map/hqk,qhe->khe/dot_general | solution.py:564
  219.3 4.0 %multiply_reduce_fusion = (f32[4,640]{1,0:T(4,128)S(1)}, f32[4,640,640]{1,2,0:T(8,128)}) fusion(f32[4,640,640]{1,2,0:T(8,128)S(1)} %bitcast.136, f32[4,640]{1,0:T(4,128)S(1)} %log_add_fusion, bf16[640,4,64]{0,2,1:T(8,128)(2,1)S(1)} %bitcast.149, f32[640,4,64]{0,2,1:T(8,128)S(1)} %bitcast.147, f32[4,64]{1,0:T(4,128)S(1)} %add.270), kind=kOutput, calls=%fused_computation.1 | convolution fusion | flops 214955520 | bytes 14111744 | tf_op jit(solution)/shard_map/qhe,khe->hqk/dot_general | solution.py:560
  223.3 1.1 convert_reduce_fusion.1
  225.2 1.5 collective-permute-start.4
  227.3 1.1 convert_reduce_fusion
  229.7 1.4 convolution_convert_fusion.6.refs_2_
  231.1 4.2 %collective-permute-done.4 = bf16[160,1024]{1,0:T(8,128)(2,1)} collective-permute-done((bf16[160,1024]{1,0:T(8,128)(2,1)}, bf16[160,1024]{1,0:T(8,128)(2,1)}, u32[]{:S(2)}, u32[]{:S(2)}) %collective-permute-start.4) | collective-permute-done | bytes 327712 | tf_op jit(solution)/shard_map/ppermute | solution.py:62
  235.3 8.3 %collective-permute-done.3 = bf16[160,1024]{1,0:T(8,128)(2,1)} collective-permute-done((bf16[160,1024]{1,0:T(8,128)(2,1)S(1)}, bf16[160,1024]{1,0:T(8,128)(2,1)}, u32[]{:S(2)}, u32[]{:S(2)}) %collective-permute-start.3) | collective-permute-done | bytes 327712 | tf_op jit(solution)/shard_map/ppermute | solution.py:62
  243.6 6.0 %multiply_convert_fusion = bf16[4,640,640]{1,2,0:T(8,128)(2,1)S(1)} fusion(f32[4,640,640]{1,2,0:T(8,128)} %get-tuple-element.136, f32[4,640,640]{1,2,0:T(8,128)} %copy-done, f32[4,640]{1,0:T(4,128)S(1)} %get-tuple-element.135, f32[4,640]{1,0:T(4,128)S(1)} %log_add_fusion), kind=kLoop, calls=%fused_computation | loop fusion | flops 6553600 | bytes 16404480 | tf_op jit(solution)/shard_map/convert_element_type | solution.py:571
  249.6 1.2 fusion.18
  253.4 1.2 collective-permute-start.5
  254.7 3.7 %bitcast_convert_fusion = (bf16[640,1024]{1,0:T(8,128)(2,1)}, f32[640,1024,1]{1,0,2:T(8,128)S(1)}) fusion(bf16[3,1024,256]{2,1,0:T(8,128)(2,1)} %get-tuple-element.45, bf16[1,640,256]{2,1,0:T(8,128)(2,1)S(1)} %copy-done.26, bf16[1,640,256]{2,1,0:T(8,128)(2,1)S(1)} %copy.34, bf16[1,640,256]{2,1,0:T(8,128)(2,1)S(1)} %copy.33), kind=kOutput, calls=%fused_computation.20 | convolution fusion | flops 1008271360 | bytes 6488064 | tf_op jit(solution)/shard_map/cpe,cde->pd/dot_general | solution.py:601
  259.9 3.7 %fusion.14.refs_1_ = bf16[3,1024,256]{2,1,0:T(8,128)(2,1)} fusion(bf16[640,1024]{1,0:T(8,128)(2,1)S(1)} %copy-done.17, bf16[1,640,256]{2,1,0:T(8,128)(2,1)S(1)} %copy-done.26, bf16[1,640,256]{2,1,0:T(8,128)(2,1)} %copy-done.28, bf16[1,640,256]{2,1,0:T(8,128)(2,1)} %copy-done.27), kind=kOutput, calls=%fused_computation.52 | convolution fusion | flops 1008402432 | bytes 3866624 | tf_op jit(solution)/shard_map/pd,cpe->cde/dot_general | solution.py:591
  263.5 7.0 %collective-permute-done.5 = bf16[160,1024]{1,0:T(8,128)(2,1)} collective-permute-done((bf16[160,1024]{1,0:T(8,128)(2,1)}, bf16[160,1024]{1,0:T(8,128)(2,1)}, u32[]{:S(2)}, u32[]{:S(2)}) %collective-permute-start.5) | collective-permute-done | bytes 327712 | tf_op jit(solution)/shard_map/ppermute | solution.py:62
  270.5 35.3 %sum_third.1 = (bf16[4,160,1024]{2,1,0:T(8,128)(2,1)}, bf16[8,3,128,256]{3,2,1,0:T(8,128)(2,1)}, bf16[8,256,128]{2,1,0:T(8,128)(2,1)}, f32[4,16,128]{2,1,0:T(8,128)}) custom-call(bf16[4,160,1024]{2,1,0:T(8,128)(2,1)} %bitcast.154, bf16[3,1024,256]{2,1,0:T(8,128)(2,1)} %fusion.14.refs_1_, bf16[256,1024]{1,0:T(8,128)(2,1)} %convolution_convert_fusion.6.refs_2_, ...), custom_call_target="tpu_custom_call" | custom-call | bytes 6815744 | tf_op jit(solution)/shard_map/sum_third/pallas_call | solution.py:334
  308.3 1.6 convert_reduce_fusion.5
  310.0 1.8 convert_reduce_fusion.9
  311.7 1.1 convert_element_type.286
  312.9 1.0 convert_reduce_fusion.4
  314.3 1.4 copy.38
  315.7 2.0 fusion.34
  (142 shorter events, 18.2 us)
Async XLA Ops:
  0.6 37.6 %copy-start.5 = (bf16[145,1,1024]{2,0,1:T(8,128)(2,1)S(1)}, bf16[145,1,1024]{2,0,1:T(8,128)(2,1)}, u32[]{:S(2)}) copy-start(bf16[145,1,1024]{2,0,1:T(8,128)(2,1)} %param.14) | copy-start | bytes 890884
  2.5 48.6 %copy-start.8 = (bf16[160,1024]{1,0:T(8,128)(2,1)}, bf16[160,1024]{1,0:T(8,128)(2,1)S(1)}, u32[]{:S(2)}) copy-start(bf16[160,1024]{1,0:T(8,128)(2,1)S(1)} %pad.89) | copy-start | bytes 983044
  35.6 6.2 %copy-start.30 = (bf16[128,128]{1,0:T(8,128)(2,1)S(1)}, bf16[128,128]{1,0:T(8,128)(2,1)}, u32[]{:S(2)}) copy-start(bf16[128,128]{1,0:T(8,128)(2,1)} %get-tuple-element.48) | copy-start | bytes 98308
  35.6 6.3 %copy-start.1 = (bf16[4,160,1024]{2,1,0:T(8,128)(2,1)S(1)}, bf16[4,160,1024]{2,1,0:T(8,128)(2,1)}, u32[]{:S(2)}) copy-start(bf16[4,160,1024]{2,1,0:T(8,128)(2,1)} %get-tuple-element.47) | copy-start | bytes 3932164
  35.6 18.0 %collective-permute-start.2 = (bf16[160,1024]{1,0:T(8,128)(2,1)S(1)}, bf16[160,1024]{1,0:T(8,128)(2,1)S(1)}, u32[]{:S(2)}, u32[]{:S(2)}) collective-permute-start(bf16[160,1024]{1,0:T(8,128)(2,1)S(1)} %pad.89), channel_id=1, source_target_pairs={{0,3},{1,0},{2,1},{3,2},{4,7},{5,4},{6,5},{7,6},{8,11},{9,8},{10,9... | collective-permute-start | bytes 983048 | tf_op jit(solution)/shard_map/ppermute | solution.py:62
  37.1 28.2 %collective-permute-start.1 = (bf16[160,1024]{1,0:T(8,128)(2,1)S(1)}, bf16[160,1024]{1,0:T(8,128)(2,1)S(1)}, u32[]{:S(2)}, u32[]{:S(2)}) collective-permute-start(bf16[160,1024]{1,0:T(8,128)(2,1)S(1)} %pad.89), channel_id=1, source_target_pairs={{0,2},{1,3},{2,0},{3,1},{4,6},{5,7},{6,4},{7,5},{8,10},{9,11},{10,... | collective-permute-start | bytes 983048 | tf_op jit(solution)/shard_map/ppermute | solution.py:62
  37.7 27.7 %collective-permute-start = (bf16[160,1024]{1,0:T(8,128)(2,1)S(1)}, bf16[160,1024]{1,0:T(8,128)(2,1)S(1)}, u32[]{:S(2)}, u32[]{:S(2)}) collective-permute-start(bf16[160,1024]{1,0:T(8,128)(2,1)S(1)} %pad.89), channel_id=1, source_target_pairs={{0,1},{1,2},{2,3},{3,0},{4,5},{5,6},{6,7},{7,4},{8,9},{9,10},{10,1... | collective-permute-start | bytes 983048 | tf_op jit(solution)/shard_map/ppermute | solution.py:62
  42.0 1.4 copy-start.33
  42.5 2.3 copy-start.16
  44.9 2.2 copy-start.6
  45.0 2.1 copy-start.3
  45.0 3.0 copy-start.10
  47.1 2.7 copy-start
  49.8 2.2 copy-start.25
  51.1 46.0 %copy-start.23 = (bf16[4,64,640]{2,1,0:T(8,128)(2,1)}, bf16[4,64,640]{2,1,0:T(8,128)(2,1)S(1)}, u32[]{:S(2)}) copy-start(bf16[4,64,640]{2,1,0:T(8,128)(2,1)S(1)} %fusion.22) | copy-start | bytes 983044
  97.1 28.3 %copy-start.29 = (bf16[640,1024]{1,0:T(8,128)(2,1)S(1)}, bf16[640,1024]{1,0:T(8,128)(2,1)}, u32[]{:S(2)}) copy-start(bf16[640,1024]{1,0:T(8,128)(2,1)} %constant_dynamic-update-slice_fusion.3) | copy-start | bytes 3932164
  125.6 3.7 %copy-start.32 = (bf16[1024,1024]{1,0:T(8,128)(2,1)S(1)}, bf16[1024,1024]{1,0:T(8,128)(2,1)}, u32[]{:S(2)}) copy-start(bf16[1024,1024]{1,0:T(8,128)(2,1)} %get-tuple-element.57) | copy-start | bytes 6291460
  140.3 3.2 %copy-start.31 = (bf16[1024,1024]{1,0:T(8,128)(2,1)S(1)}, bf16[1024,1024]{1,0:T(8,128)(2,1)}, u32[]{:S(2)}) copy-start(bf16[1024,1024]{1,0:T(8,128)(2,1)} %get-tuple-element.53) | copy-start | bytes 6291460
  143.5 2.6 copy-start.21
  176.6 2.3 copy-start.9
  179.0 40.3 %slice-start = ((s8[6553600]{0:T(1024)(128)(4,1)}), s8[2359296]{0:T(1024)(128)(4,1)S(1)}, s32[]{:S(2)}) async-start(s8[6553600]{0:T(1024)(128)(4,1)} %bitcast.135), calls=%async_computation | async-start | bytes 4718592
  212.2 7.1 %slice-start.1 = ((s8[6553600]{0:T(1024)(128)(4,1)}), s8[4194304]{0:T(1024)(128)(4,1)S(1)}, s32[]{:S(2)}) async-start(s8[6553600]{0:T(1024)(128)(4,1)} %bitcast.135), calls=%async_computation.1 | async-start | bytes 8388608
  214.4 4.9 %copy-start.11 = (f32[1,640,256]{1,2,0:T(8,128)S(1)}, f32[1,640,256]{1,2,0:T(8,128)}, u32[]{:S(2)}) copy-start(f32[1,640,256]{1,2,0:T(8,128)} %copy-done.10) | copy-start | bytes 1966084
  219.3 4.0 %copy-start.13 = (bf16[8,128,1024]{2,1,0:T(8,128)(2,1)S(1)}, bf16[8,128,1024]{2,1,0:T(8,128)(2,1)}, u32[]{:S(2)}) copy-start(bf16[8,128,1024]{2,1,0:T(8,128)(2,1)} %get-tuple-element.74) | copy-start | bytes 6291460
  219.3 5.2 %copy-start.18 = (bf16[640,1024]{1,0:T(8,128)(2,1)S(1)}, bf16[640,1024]{1,0:T(8,128)(2,1)}, u32[]{:S(2)}) copy-start(bf16[640,1024]{1,0:T(8,128)(2,1)} %convolution_convert_fusion.4) | copy-start | bytes 3932164
  223.3 4.0 %copy-start.14 = (bf16[8,1024,128]{2,1,0:T(8,128)(2,1)S(1)}, bf16[8,1024,128]{2,1,0:T(8,128)(2,1)}, u32[]{:S(2)}) copy-start(bf16[8,1024,128]{2,1,0:T(8,128)(2,1)} %get-tuple-element.75) | copy-start | bytes 6291460
  224.5 4.2 %copy-start.22 = (bf16[4,64,640]{2,1,0:T(8,128)(2,1)S(1)}, bf16[4,64,640]{2,1,0:T(8,128)(2,1)}, u32[]{:S(2)}) copy-start(bf16[4,64,640]{2,1,0:T(8,128)(2,1)} %get-tuple-element.140) | copy-start | bytes 983044
  224.5 5.3 %copy-start.20 = (bf16[4,160,1024]{2,1,0:T(8,128)(2,1)S(1)}, bf16[4,160,1024]{2,1,0:T(8,128)(2,1)}, u32[]{:S(2)}) copy-start(bf16[4,160,1024]{2,1,0:T(8,128)(2,1)} %get-tuple-element.60) | copy-start | bytes 3932164
  224.5 5.3 %copy-start.24 = (bf16[4,64,640]{2,1,0:T(8,128)(2,1)S(1)}, bf16[4,64,640]{2,1,0:T(8,128)(2,1)}, u32[]{:S(2)}) copy-start(bf16[4,64,640]{2,1,0:T(8,128)(2,1)} %copy-done.23) | copy-start | bytes 983044
  225.2 10.1 %collective-permute-start.4 = (bf16[160,1024]{1,0:T(8,128)(2,1)}, bf16[160,1024]{1,0:T(8,128)(2,1)}, u32[]{:S(2)}, u32[]{:S(2)}) collective-permute-start(bf16[160,1024]{1,0:T(8,128)(2,1)} %get-tuple-element.112), channel_id=1, source_target_pairs={{0,3},{1,0},{2,1},{3,2},{4,7},{5,4},{6,5},{7,6},{8,11},{9,8},{10,9... | collective-permute-start | bytes 983048 | tf_op jit(solution)/shard_map/ppermute | solution.py:62
  226.8 16.8 %collective-permute-start.3 = (bf16[160,1024]{1,0:T(8,128)(2,1)S(1)}, bf16[160,1024]{1,0:T(8,128)(2,1)}, u32[]{:S(2)}, u32[]{:S(2)}) collective-permute-start(bf16[160,1024]{1,0:T(8,128)(2,1)S(1)} %get-tuple-element.113), channel_id=1, source_target_pairs={{0,1},{1,2},{2,3},{3,0},{4,5},{5,6},{6,7},{7,4},{8,9},{9,10},{10,1... | collective-permute-start | bytes 983048 | tf_op jit(solution)/shard_map/ppermute | solution.py:62
  243.6 6.0 %copy-start.4 = (f32[1,640,256]{1,2,0:T(8,128)S(1)}, f32[1,640,256]{1,2,0:T(8,128)}, u32[]{:S(2)}) copy-start(f32[1,640,256]{1,2,0:T(8,128)} %copy-done.3) | copy-start | bytes 1966084
  249.6 1.2 copy-start.7
  250.8 1.3 copy-start.19
  250.8 3.8 %copy-start.26 = (bf16[1,640,256]{2,1,0:T(8,128)(2,1)S(1)}, bf16[1,640,256]{2,1,0:T(8,128)(2,1)}, u32[]{:S(2)}) copy-start(bf16[1,640,256]{2,1,0:T(8,128)(2,1)} %copy.35) | copy-start | bytes 983044
  253.2 1.5 copy-start.27
  253.4 1.3 copy-start.28
  253.4 5.0 %copy-start.2 = (bf16[4,160,1024]{2,1,0:T(8,128)(2,1)S(1)}, bf16[4,160,1024]{2,1,0:T(8,128)(2,1)}, u32[]{:S(2)}) copy-start(bf16[4,160,1024]{2,1,0:T(8,128)(2,1)} %get-tuple-element.47) | copy-start | bytes 3932164
  253.4 17.1 %collective-permute-start.5 = (bf16[160,1024]{1,0:T(8,128)(2,1)}, bf16[160,1024]{1,0:T(8,128)(2,1)}, u32[]{:S(2)}, u32[]{:S(2)}) collective-permute-start(bf16[160,1024]{1,0:T(8,128)(2,1)} %get-tuple-element.111), channel_id=1, source_target_pairs={{0,2},{1,3},{2,0},{3,1},{4,6},{5,7},{6,4},{7,5},{8,10},{9,11},{10,... | collective-permute-start | bytes 983048 | tf_op jit(solution)/shard_map/ppermute | solution.py:62
  258.4 1.5 copy-start.17
  306.6 6.2 %copy-start.15 = (bf16[8,3,128,256]{3,2,1,0:T(8,128)(2,1)S(1)}, bf16[8,3,128,256]{3,2,1,0:T(8,128)(2,1)}, u32[]{:S(2)}) copy-start(bf16[8,3,128,256]{3,2,1,0:T(8,128)(2,1)} %get-tuple-element.72) | copy-start | bytes 4718596
  311.7 2.4 copy-start.12
